TPU v7x, 256 devices: a whole 4x4x8 slice. The times are simulated.
256 devices in a mesh: frames: 64 (over z, x, core), mp: 4 (over y).
Axes of the slice: x: 4, y: 4, z: 8, core: 2. Of those that a mesh axis runs over, the one named last changes fastest.
Arguments:
- video_tokens: bfloat16 [64, 256, 1024], P('frames', 'mp'), may hold values from -64 to 64
- grad_output: bfloat16 [64, 256, 1024], P('frames', 'mp'), may hold values from -16 to 16
- spatial_qkv: bfloat16 [3, 1024, 1024], P(None, None, 'mp'), may hold values from -1 to 1
- spatial_out: bfloat16 [1024, 1024], P('mp'), may hold values from -0.1875 to 0.1875
- temporal_qkv: bfloat16 [3, 1024, 1024], P(None, None, 'mp'), may hold values from -1 to 1
- temporal_out: bfloat16 [1024, 1024], P('mp'), may hold values from -0.1875 to 0.1875
- clip_frames: int32 [32], replicated, may hold values from 1 to 4, 64 in all
Outputs:
- grad_tokens: bfloat16 [64, 256, 1024], P('frames', 'mp')
- grad_spatial_qkv: float32 [3, 1024, 1024], P(None, 'frames', 'mp')
- grad_spatial_out: float32 [1024, 1024], P('mp', 'frames')
- grad_temporal_qkv: float32 [3, 1024, 1024], P(None, 'frames', 'mp')
- grad_temporal_out: float32 [1024, 1024], P('mp', 'frames')
Inputs may be any that keep to these rules, and one draw needn't show every extreme that they name: `clip_frames`: 32 clip lengths that sum to 64; the longest is exactly 4.
All inputs are finite; a program needn't handle non-finite values.
Results may differ from a plain program's by a relative error of at most 0.015.
Values may be sent and summed in bfloat16 or wider, within the bound.
A program may use at most 128 MiB of HBM per device.

v0:
```python
import jax
import jax.numpy as jnp
from jax import lax
from jax.sharding import PartitionSpec as P

HD = 64


EPS = 1e-06
NEGATIVE = -1e30


def normed(values_in):
    inv_rms = lax.rsqrt(jnp.mean(values_in * values_in, -1, keepdims=True) + EPS)
    return ((values_in * inv_rms).astype(jnp.bfloat16), inv_rms)


def norm_back(values_in, inv_rms, upstream):
    return inv_rms * (
        upstream
        - values_in * (inv_rms * inv_rms) * jnp.mean(upstream * values_in, -1, keepdims=True)
    )


def probs_of(queries, keys_in, mask_bias, layout):
    key_layout = layout.replace("l", "m")
    scores = jnp.einsum(
        layout + "," + key_layout + "->bhlm", queries, keys_in, preferred_element_type=jnp.float32
    )
    scores = scores * queries.shape[-1] ** (-0.5) + mask_bias
    scores = scores - jnp.max(scores, -1, keepdims=True)
    expo = jnp.exp(scores)
    return expo / jnp.sum(expo, -1, keepdims=True)


def attend(queries, keys_in, values_in, mask_bias, layout):
    key_layout = layout.replace("l", "m")
    probs_f = probs_of(queries, keys_in, mask_bias, layout)
    result = jnp.einsum(
        "bhlm," + key_layout + "->" + layout,
        probs_f.astype(jnp.bfloat16),
        values_in,
        preferred_element_type=jnp.float32,
    )
    return result.astype(jnp.bfloat16)


def attend_back(queries, keys_in, values_in, mask_bias, upstream, layout):
    key_layout = layout.replace("l", "m")
    probs_f = probs_of(queries, keys_in, mask_bias, layout)
    d_values = jnp.einsum(
        "bhlm," + layout + "->" + key_layout,
        probs_f.astype(jnp.bfloat16),
        upstream,
        preferred_element_type=jnp.float32,
    )
    d_probs = jnp.einsum(
        layout + "," + key_layout + "->bhlm",
        upstream,
        values_in,
        preferred_element_type=jnp.float32,
    )
    row_delta = jnp.sum(probs_f * d_probs, -1, keepdims=True)
    d_scores = (probs_f * (d_probs - row_delta) * queries.shape[-1] ** (-0.5)).astype(jnp.bfloat16)
    d_queries = jnp.einsum(
        "bhlm," + key_layout + "->" + layout, d_scores, keys_in, preferred_element_type=jnp.float32
    )
    d_keys = jnp.einsum(
        "bhlm," + layout + "->" + key_layout, d_scores, queries, preferred_element_type=jnp.float32
    )
    return (d_queries, d_keys, d_values)


def shards(
    video_tokens, grad_output, spatial_qkv, spatial_out, temporal_qkv, temporal_out, clip_frames
):
    frames_dev, rows_mp, model_width = video_tokens.shape
    local_width = spatial_out.shape[0]
    heads_loc = local_width // HD
    groups = lax.axis_size("frames")
    patches = rows_mp * lax.axis_size("mp")
    all_frames = frames_dev * groups
    tokens = frames_dev * patches

    def patch_rows(tensor):
        return lax.all_gather(tensor, "mp", axis=1, tiled=True)

    def heads_of(tensor):
        return tensor.reshape(tensor.shape[:-1] + (heads_loc, HD))

    def patch_sums(tensor):
        return lax.psum_scatter(
            tensor.reshape(frames_dev, patches, model_width), "mp", scatter_dimension=1, tiled=True
        )

    def back_sum(d_flat, weights_local):
        return patch_sums(
            jnp.einsum("jne,jde->nd", d_flat, weights_local, preferred_element_type=jnp.float32)
        )

    clip_ends = jnp.cumsum(clip_frames)
    x_float = video_tokens.astype(jnp.float32)
    normed_x, inv_x = normed(x_float)
    normed_x_all = patch_rows(normed_x).reshape(tokens, model_width)
    qkv_s = jnp.einsum(
        "nd,jde->jne", normed_x_all, spatial_qkv, preferred_element_type=jnp.float32
    ).astype(jnp.bfloat16)
    qkv_s = qkv_s.reshape(3, frames_dev, patches, heads_loc, HD)
    attn_s = attend(qkv_s[0], qkv_s[1], qkv_s[2], 0.0, "blhd").reshape(tokens, local_width)
    hidden = x_float + patch_sums(jnp.dot(attn_s, spatial_out, preferred_element_type=jnp.float32))
    normed_h, inv_h = normed(hidden)
    normed_h_all = patch_rows(normed_h).reshape(tokens, model_width)
    qkv_t = jnp.einsum(
        "nd,jde->jne", normed_h_all, temporal_qkv, preferred_element_type=jnp.float32
    ).astype(jnp.bfloat16)
    qkv_t = qkv_t.reshape(3, frames_dev, patches, local_width)
    grad_all = patch_rows(grad_output).reshape(tokens, model_width)

    def to_owners(tensor):
        return lax.all_to_all(tensor, "frames", split_axis=2, concat_axis=1, tiled=True)

    def from_owners(tensor):
        return lax.all_to_all(tensor, "frames", split_axis=1, concat_axis=2, tiled=True)

    at_owners = to_owners(qkv_t)
    clip_ids = jnp.sum(
        (jnp.arange(all_frames, dtype=jnp.int32)[:, None] >= clip_ends[None, :]).astype(jnp.int32),
        axis=1,
    )
    mask_bias = jnp.where(clip_ids[:, None] == clip_ids[None, :], 0.0, NEGATIVE).astype(jnp.float32)
    own_queries = heads_of(at_owners[0])
    own_keys = heads_of(at_owners[1])
    own_values = heads_of(at_owners[2])
    attn_owned = attend(own_queries, own_keys, own_values, mask_bias, "lbhd")
    attn_t = from_owners(attn_owned.reshape((1,) + at_owners.shape[1:]))[0].reshape(
        tokens, local_width
    )
    d_attn_t = jnp.einsum(
        "nd,ed->ne", grad_all, temporal_out, preferred_element_type=jnp.float32
    ).astype(jnp.bfloat16)
    d_owned = to_owners(d_attn_t.reshape(1, frames_dev, patches, local_width))[0]
    d_queries, d_keys, d_values = attend_back(
        own_queries, own_keys, own_values, mask_bias, heads_of(d_owned), "lbhd"
    )
    d_stack = jnp.stack([d_queries, d_keys, d_values]).astype(jnp.bfloat16).reshape(at_owners.shape)
    d_qkv_t = from_owners(d_stack)
    grad_temporal_out = jnp.einsum(
        "ne,nd->ed", attn_t, grad_all, preferred_element_type=jnp.float32
    )
    d_qkv_t_flat = d_qkv_t.reshape(3, tokens, local_width)
    grad_temporal_qkv = jnp.einsum(
        "nd,jne->jde", normed_h_all, d_qkv_t_flat, preferred_element_type=jnp.float32
    )
    d_normed_h = back_sum(d_qkv_t_flat, temporal_qkv)
    d_hidden = grad_output.astype(jnp.float32) + norm_back(hidden, inv_h, d_normed_h)
    d_hidden_all = patch_rows(d_hidden.astype(jnp.bfloat16)).reshape(tokens, model_width)
    grad_spatial_out = jnp.einsum(
        "ne,nd->ed", attn_s, d_hidden_all, preferred_element_type=jnp.float32
    )
    d_attn_s = jnp.einsum(
        "nd,ed->ne", d_hidden_all, spatial_out, preferred_element_type=jnp.float32
    ).astype(jnp.bfloat16)
    d_attn_s = d_attn_s.reshape(frames_dev, patches, heads_loc, HD)
    d_queries_s, d_keys_s, d_values_s = attend_back(
        qkv_s[0], qkv_s[1], qkv_s[2], 0.0, d_attn_s, "blhd"
    )
    d_qkv_s = (
        jnp.stack([d_queries_s, d_keys_s, d_values_s])
        .astype(jnp.bfloat16)
        .reshape(3, tokens, local_width)
    )
    grad_spatial_qkv = jnp.einsum(
        "nd,jne->jde", normed_x_all, d_qkv_s, preferred_element_type=jnp.float32
    )
    d_normed_x = back_sum(d_qkv_s, spatial_qkv)
    grad_tokens = (d_hidden + norm_back(x_float, inv_x, d_normed_x)).astype(jnp.bfloat16)
    reduced = (
        lax.psum_scatter(grad_spatial_qkv, "frames", scatter_dimension=1, tiled=True),
        lax.psum_scatter(grad_spatial_out, "frames", scatter_dimension=1, tiled=True),
        lax.psum_scatter(grad_temporal_qkv, "frames", scatter_dimension=1, tiled=True),
        lax.psum_scatter(grad_temporal_out, "frames", scatter_dimension=1, tiled=True),
    )
    return (grad_tokens, reduced[0], reduced[1], reduced[2], reduced[3])


def solution(mesh):
    placed = (
        P("frames", "mp", None),
        P("frames", "mp", None),
        P(None, None, "mp"),
        P("mp", None),
        P(None, None, "mp"),
        P("mp", None),
        P(),
    )
    return jax.shard_map(
        shards,
        mesh=mesh,
        in_specs=placed,
        out_specs=(
            P("frames", "mp", None),
            P(None, "frames", "mp"),
            P("mp", "frames"),
            P(None, "frames", "mp"),
            P("mp", "frames"),
        ),
        check_vma=False,
    )
```

profile of v0, /device:TPU:8, one launch (start us, length us, event | category | flops | bytes accessed | tf_op | source)
XLA Modules:
  0.0 722.4 jit_solution(7980183835624135198)
XLA Ops:
  9.9 13.7 %all_gather.12 = bf16[1,256,1024]{2,1,0:T(8,128)(2,1)S(1)} all-gather(bf16[1,64,1024]{2,1,0:T(8,128)(2,1)S(1)} %fusion.41), channel_id=1, replica_groups=mesh['frames'=64,'mp'=4] {'mp'}, dimensions={1}, use_global_device_ids=true | all-gather | bytes 655360 | tf_op jit(solution)/shard_map/all_gather | solution.py:86
  23.6 2.3 fusion.17
  26.0 1.5 fusion.70
  29.9 12.9 %all_gather.14 = bf16[1,256,1024]{2,1,0:T(8,128)(2,1)S(1)} all-gather(bf16[1,64,1024]{2,1,0:T(8,128)(2,1)S(1)} %copy-done.13), channel_id=1, replica_groups=mesh['frames'=64,'mp'=4] {'mp'}, dimensions={1}, use_global_device_ids=true | all-gather | bytes 655360 | tf_op jit(solution)/shard_map/all_gather | solution.py:86
  43.9 1.4 reduce.19
  46.1 12.6 %all-to-all-start.1 = ((bf16[64,2,512]{2,1,0:T(2,128)(2,1)}), bf16[64,2,512]{2,1,0:T(2,128)(2,1)S(1)}, u32[]{:S(2)}, u32[]{:S(2)}) async-start(bf16[64,2,512]{2,1,0:T(2,128)(2,1)} %reshape.319), calls=%async_computation.2 | async-start | bytes 262144 | tf_op jit(solution)/shard_map/all_to_all | solution.py:120
  61.4 13.4 %all_gather.13 = bf16[1,256,1024]{2,1,0:T(8,128)(2,1)S(1)} all-gather(bf16[1,64,1024]{2,1,0:T(8,128)(2,1)S(1)} %multiply_convert_fusion), channel_id=1, replica_groups=mesh['frames'=64,'mp'=4] {'mp'}, dimensions={1}, use_global_device_ids=true | all-gather | bytes 655360 | tf_op jit(solution)/shard_map/all_gather | solution.py:86
  77.4 10.3 %all-to-all-start = ((bf16[3,1,256,256]{3,0,1,2:T(4,128)(2,1)}), bf16[3,1,256,256]{3,0,1,2:T(4,128)(2,1)S(1)}, u32[]{:S(2)}, u32[]{:S(2)}) async-start(bf16[3,1,256,256]{3,0,1,2:T(4,128)(2,1)} %copy.131), calls=%async_computation.1 | async-start | bytes 1048576 | tf_op jit(solution)/shard_map/all_to_all | solution.py:120
  90.2 15.1 %all-to-all-done = bf16[3,1,256,256]{3,0,1,2:T(4,128)(2,1)S(1)} async-done(((bf16[3,1,256,256]{3,0,1,2:T(4,128)(2,1)}), bf16[3,1,256,256]{3,0,1,2:T(4,128)(2,1)S(1)}, u32[]{:S(2)}, u32[]{:S(2)}) %all-to-all-start) | async-done | bytes 393248 | tf_op jit(solution)/shard_map/all_to_all | solution.py:120
  105.3 2.3 slice_reduce_fusion
  113.0 2.6 convolution_convert_fusion.4
  115.7 1.9 convolution_convert_fusion.5
  120.3 20.5 %all_to_all.16 = bf16[3,64,4,256]{3,2,0,1:T(4,128)(2,1)S(1)} all-to-all(bf16[3,64,4,256]{3,2,0,1:T(4,128)(2,1)S(1)} %pad_maximum_fusion), channel_id=1, replica_groups=mesh['frames'=64,'mp'=4] {'frames'}, dimensions={1} | all-to-all | bytes 786432 | tf_op jit(solution)/shard_map/all_to_all | solution.py:123
  141.0 1.6 convolution_bitcast_fusion.3
  142.7 20.5 %reduce-scatter.8.cloned.1.call-done = f32[1,64,1024]{2,1,0:T(8,128)} async-done(((f32[1,256,1024]{2,1,0:T(8,128)}), f32[1,64,1024]{2,1,0:T(8,128)}) %reduce-scatter.8.cloned.1.call-update) | async-done | bytes 262160 | tf_op jit(solution)/shard_map/reduce_scatter | solution.py:92
  164.4 1.8 fusion.68
  166.2 13.5 %all_gather.15 = bf16[1,256,1024]{2,1,0:T(8,128)(2,1)S(1)} all-gather(bf16[1,64,1024]{2,1,0:T(8,128)(2,1)S(1)} %get-tuple-element.35), channel_id=1, replica_groups=mesh['frames'=64,'mp'=4] {'mp'}, dimensions={1}, use_global_device_ids=true | all-gather | bytes 655360 | tf_op jit(solution)/shard_map/all_gather | solution.py:86
  181.1 1.7 convolution_convert_fusion.6
  182.8 1.4 fusion.73
  184.2 3.4 convolution_convert_fusion.8
  187.6 2.6 convolution_convert_fusion.7
  191.5 3.1 convolution_bitcast_fusion.2
  194.8 3.3 convolution_bitcast_fusion
  198.1 5.0 copy.157
  203.2 3.3 convolution_bitcast_fusion.1
  206.4 5.0 copy.155
  212.5 1.5 convolution_convert_fusion.2
  214.1 21.3 %all_to_all.17 = bf16[1,64,4,256]{3,2,0,1:T(4,128)(2,1)S(1)} all-to-all(bf16[1,64,4,256]{3,2,0,1:T(4,128)(2,1)S(1)} %copy.160), channel_id=1, replica_groups=mesh['frames'=64,'mp'=4] {'frames'}, dimensions={1} | all-to-all | bytes 262144 | tf_op jit(solution)/shard_map/all_to_all | solution.py:123
  240.7 1.7 fusion.46
  242.4 188.5 %all-reduce.5.cloned.1.call-done = (f32[3,1024,256]{2,0,1:T(4,128)}, f32[3,1024,256]{2,0,1:T(4,128)}) async-done(((f32[3,1024,256]{2,0,1:T(4,128)}, f32[3,1024,256]{2,0,1:T(4,128)}), (f32[3,1024,256]{2,0,1:T(4,128)}, f32[3,1024,256]{2,0,1:T(4,128)})) %all-reduce.5.cloned.1.call-update) | async-done | bytes 6291472
  433.1 140.4 %reduce-scatter.14.cloned.1.call-done = f32[256,16]{0,1:T(8,128)} async-done(((f32[256,1024]{0,1:T(8,128)}), f32[256,16]{0,1:T(8,128)}) %reduce-scatter.14.cloned.1.call-update) | async-done | bytes 16400 | tf_op jit(solution)/shard_map/reduce_scatter | solution.py:181
  573.5 142.1 %reduce-scatter.12.cloned.1.call-done = f32[256,16]{0,1:T(8,128)} async-done(((f32[256,1024]{0,1:T(8,128)}), f32[256,16]{0,1:T(8,128)}) %reduce-scatter.12.cloned.1.call-update) | async-done | bytes 16400 | tf_op jit(solution)/shard_map/reduce_scatter | solution.py:179
  (133 shorter events, 34.8 us)
Async XLA Ops:
  7.2 68.4 %copy-start = (bf16[3,1024,256]{2,1,0:T(8,128)(2,1)S(1)}, bf16[3,1024,256]{2,1,0:T(8,128)(2,1)}, u32[]{:S(2)}) copy-start(bf16[3,1024,256]{2,1,0:T(8,128)(2,1)} %param.11) | copy-start | bytes 4718596
  7.2 51.5 %reduce-scatter.6.cloned.1.call-start = ((), (), s32[]{:S(2)}) async-start(), calls=%async_computation.9 | async-start | bytes 1310720 | tf_op jit(solution)/shard_map/reduce_scatter | solution.py:92
  23.6 2.4 copy-start.5
  26.0 1.5 copy-start.22
  26.0 2.2 copy-start.17
  26.0 2.2 copy-start.24
  28.2 14.6 %copy-start.19 = (bf16[4,64,256]{2,1,0:T(8,128)(2,1)}, bf16[4,64,256]{2,1,0:T(8,128)(2,1)S(1)}, u32[]{:S(2)}) copy-start(bf16[4,64,256]{2,1,0:T(8,128)(2,1)S(1)} %convolution_convert_fusion.11) | copy-start | bytes 393220
  28.2 1.7 copy-start.13
  28.5 14.3 %copy-start.16 = (bf16[256,1024]{1,0:T(8,128)(2,1)S(1)}, bf16[256,1024]{1,0:T(8,128)(2,1)}, u32[]{:S(2)}) copy-start(bf16[256,1024]{1,0:T(8,128)(2,1)} %param.12) | copy-start | bytes 1572868
  29.9 28.8 %copy-start.1 = (bf16[1,64,1024]{2,1,0:T(8,128)(2,1)S(1)}, bf16[1,64,1024]{2,1,0:T(8,128)(2,1)}, u32[]{:S(2)}) copy-start(bf16[1,64,1024]{2,1,0:T(8,128)(2,1)} %param.7) | copy-start | bytes 393220
  46.1 31.3 %all-to-all-start.1 = ((bf16[64,2,512]{2,1,0:T(2,128)(2,1)}), bf16[64,2,512]{2,1,0:T(2,128)(2,1)S(1)}, u32[]{:S(2)}, u32[]{:S(2)}) async-start(bf16[64,2,512]{2,1,0:T(2,128)(2,1)} %reshape.319), calls=%async_computation.2 | async-start | bytes 262144 | tf_op jit(solution)/shard_map/all_to_all | solution.py:120
  76.2 11.7 %copy-start.26 = (s32[32]{0:T(128)S(1)}, s32[32]{0:T(128)}, u32[]{:S(2)}) copy-start(s32[32]{0:T(128)} %param.13) | copy-start | bytes 388
  77.4 27.9 %all-to-all-start = ((bf16[3,1,256,256]{3,0,1,2:T(4,128)(2,1)}), bf16[3,1,256,256]{3,0,1,2:T(4,128)(2,1)S(1)}, u32[]{:S(2)}, u32[]{:S(2)}) async-start(bf16[3,1,256,256]{3,0,1,2:T(4,128)(2,1)} %copy.131), calls=%async_computation.1 | async-start | bytes 1048576 | tf_op jit(solution)/shard_map/all_to_all | solution.py:120
  87.6 75.6 %reduce-scatter.8.cloned.1.call-start = ((), (), s32[]{:S(2)}) async-start(), calls=%async_computation.10 | async-start | bytes 1310720 | tf_op jit(solution)/shard_map/reduce_scatter | solution.py:92
  108.0 3.9 copy-start.10
  110.9 6.7 copy-start.4
  113.0 2.6 copy-start.12
  141.0 22.3 %copy-start.2 = (f32[1,64,1024]{2,1,0:T(8,128)S(1)}, f32[1,64,1024]{2,1,0:T(8,128)}, u32[]{:S(2)}) copy-start(f32[1,64,1024]{2,1,0:T(8,128)} %reduce-scatter.6.cloned.1.call-done) | copy-start | bytes 786436
  142.7 21.7 %copy-start.14 = (bf16[1,64,1024]{2,1,0:T(8,128)(2,1)S(1)}, bf16[1,64,1024]{2,1,0:T(8,128)(2,1)}, u32[]{:S(2)}) copy-start(bf16[1,64,1024]{2,1,0:T(8,128)(2,1)} %param.8) | copy-start | bytes 393220
  142.7 21.7 %copy-start.25 = (f32[64]{0:T(128)S(1)}, f32[64]{0:T(128)}, u32[]{:S(2)}) copy-start(f32[64]{0:T(128)} %get-tuple-element.42) | copy-start | bytes 772
  142.7 96.8 %reduce-scatter.10.cloned.1.call-start = ((), (), s32[]{:S(2)}) async-start(), calls=%async_computation.11 | async-start | bytes 1310720 | tf_op jit(solution)/shard_map/reduce_scatter | solution.py:92
  181.0 1.8 copy-start.18
  181.0 3.1 copy-start.30
  184.2 3.4 copy-start.23
  191.5 3.1 copy-start.8
  194.5 236.4 %all-reduce.5.cloned.1.call-start = ((), (), s32[]{:S(2)}) async-start(), calls=%async_computation.14 | async-start | bytes 16777216
  198.1 5.0 copy-start.6
  211.5 361.9 %reduce-scatter.14.cloned.1.call-start = ((), (), s32[]{:S(2)}) async-start(), calls=%async_computation.13 | async-start | bytes 1064960 | tf_op jit(solution)/shard_map/reduce_scatter | solution.py:181
  235.4 1.5 copy-start.20
  236.8 3.8 copy-start.9
  236.8 3.8 copy-start.27
  236.8 478.7 %reduce-scatter.12.cloned.1.call-start = ((), (), s32[]{:S(2)}) async-start(), calls=%async_computation.12 | async-start | bytes 1064960 | tf_op jit(solution)/shard_map/reduce_scatter | solution.py:179
  (7 other events, 7.1 us)
Sparse Core Ops, SparseCore 0:
  30.0 26.5 reduce-scatter.5
  142.8 20.4 reduce-scatter.7
  194.7 25.1 reduce-scatter.9
  223.9 207.0 all-reduce.4
  435.3 138.0 reduce-scatter.13
  577.9 137.6 reduce-scatter.11
where the time goes:
time: 724 us; the launch traced here: 722 us
  waiting for transfers between devices  507 us (70%)
  blocking collectives  95.2 us (13%)
  matrix products  40.6 us (6%)
  local copies, waits for them, and re-layouts  26.3 us (4%)
  starting transfers between devices  23.5 us (3%)
  between operations  15.3 us (2%)
  other arithmetic  14.7 us (2%)
    unnamed x7, waiting for transfers between devices  189 us
    reduce_scatter x1, waiting for transfers between devices, shards(): lax.psum_scatter(grad_spatial_out, 'frames', scatter_dimension=1, tiled=T...  142 us
    reduce_scatter x1, waiting for transfers between devices, shards(): lax.psum_scatter(grad_temporal_out, 'frames', scatter_dimension=1, tiled=...  140 us
    all_gather x4, blocking collectives, patch_rows(): return lax.all_gather(tensor, 'mp', axis=1, tiled=True)  53.5 us
    all_to_all x2, blocking collectives, from_owners(): lax.all_to_all(tensor, 'frames', split_axis=1, concat_axis=2, tiled=True)  41.7 us
    all_to_all x2, starting transfers between devices, to_owners(): lax.all_to_all(tensor, 'frames', split_axis=2, concat_axis=1, tiled=True)  22.8 us
    reduce_scatter x3, waiting for transfers between devices, patch_sums(): lax.psum_scatter(tensor.reshape(frames_dev, patches, model_width), 'mp',...  20.6 us
    all_to_all x2, waiting for transfers between devices, to_owners(): lax.all_to_all(tensor, 'frames', split_axis=2, concat_axis=1, tiled=True)  15.1 us
  transfers between devices with their start and end apart: 8, of which 5 were waited for; matrix products, arithmetic and copies ran while one was open for 5% of the time, Pallas kernels for 0%

commit v1 on v0

v1 whole, which is shorter than its diff:
```python
import jax
import jax.numpy as jnp
from jax import lax
from jax.experimental import pallas as pl
from jax.experimental.pallas import tpu as pltpu
from jax.sharding import PartitionSpec as P

HD = 64
EPS = 1e-06
NEGATIVE = -1e30
FR = 64
MP = 4
XS = 4
ZS = 8
D = 1024
LW = 256
ROWS = 64
HEADS_LOC = 4
MESH = pl.DeviceIdType.MESH
F32 = jnp.float32
BF16 = jnp.bfloat16


def dot(a, b):
    return lax.dot_general(a, b, (((1,), (0,)), ((), ())), preferred_element_type=F32)


def dot_bt(a, b):
    return lax.dot_general(a, b, (((1,), (1,)), ((), ())), preferred_element_type=F32)


def dot_at(a, b):
    return lax.dot_general(a, b, (((0,), (0,)), ((), ())), preferred_element_type=F32)


def head_mask(h):
    lane = lax.broadcasted_iota(jnp.int32, (1, LW), 1)
    return jnp.where(lane // HD == h, 1.0, 0.0).astype(BF16)


def softmax(scores):
    expo = jnp.exp(scores - jnp.max(scores, -1, keepdims=True))
    return expo / jnp.sum(expo, -1, keepdims=True)


def score_grads(probs, d_probs):
    delta = jnp.sum(probs * d_probs, -1, keepdims=True)
    return (probs * (d_probs - delta) * HD ** (-0.5)).astype(BF16)


def norm_back(values_in, inv_rms, upstream):
    mean = jnp.mean(upstream * values_in, -1, keepdims=True)
    return inv_rms * (upstream - values_in * (inv_rms * inv_rms) * mean)


def kernel(
    x_ref, g_ref, cf_row, cf_col, ws_hbm, wos_hbm, wt_hbm, wot_hbm,
    tok_ref, gs_ref, gso_ref, gt_ref, gto_ref,
    ws, wos, wt, wot, xall, gall, nhall, dhall,
    perm, bias, qkvs, probs, attns, dat, hid, dhid,
    rsend, rrecv, a2send, a2recv, tq, dqkv,
    gbuf, grecv1, gsum1, grecv2, gsum2, grecv3,
    w_sem, mp_send, mp_recv, a2_ssem, a2_rsem, c_send, c_recv, x_send, x_recv, z_send, z_recv,
):
    f = lax.axis_index("frames")
    m = lax.axis_index("mp")
    core = lax.rem(f, 2)
    xpos = lax.rem(f // 2, XS)
    zpos = f // (2 * XS)

    def remote(src, dst, ssem, rsem, to_f, to_m):
        return pltpu.make_async_remote_copy(
            src_ref=src, dst_ref=dst, send_sem=ssem, recv_sem=rsem,
            device_id=(to_f, to_m), device_id_type=MESH,
        )

    pending = []

    loads = [
        pltpu.make_async_copy(hbm, vmem, w_sem.at[i])
        for i, (hbm, vmem) in enumerate(
            ((ws_hbm, ws), (wos_hbm, wos), (wot_hbm, wot), (wt_hbm, wt))
        )
    ]
    for load in loads:
        load.start()

    barrier = pltpu.get_barrier_semaphore()

    def greet(step, carry):
        pl.semaphore_signal(
            barrier, inc=1, device_id=(lax.rem(f + step, FR), m), device_id_type=MESH
        )
        return carry

    for k in range(1, MP):
        pl.semaphore_signal(
            barrier, inc=1, device_id=(f, lax.rem(m + k, MP)), device_id_type=MESH
        )
    lax.fori_loop(1, FR, greet, 0)

    def gather_mp(phase, src, buf):
        copies = []
        for k in (1, 3, 2):
            copy = remote(
                src, buf.at[m], mp_send.at[phase, k - 1], mp_recv.at[phase, k - 1],
                f, lax.rem(m + k, MP),
            )
            copy.start()
            copies.append(copy)
        pending.extend(copies)
        return copies

    def scatter_mp(phase, which):
        copies = []
        for k in (1, 3, 2):
            to = lax.rem(m + k, MP)
            copy = remote(
                rsend.at[which, to], rrecv.at[which, k - 1],
                mp_send.at[phase, k - 1], mp_recv.at[phase, k - 1], f, to,
            )
            copy.start()
            copies.append(copy)
        pending.extend(copies)
        return copies

    x = x_ref[...].astype(F32)
    inv_x = lax.rsqrt(jnp.mean(x * x, -1, keepdims=True) + EPS)
    xall[m] = (x * inv_x).astype(BF16)
    gall[m] = g_ref[...]
    pl.semaphore_wait(barrier, FR - 1 + MP - 1)

    ag_x = gather_mp(0, xall.at[m], xall)
    ag_g = gather_mp(1, g_ref, gall)

    row = lax.broadcasted_iota(jnp.int32, (LW, LW), 0)
    col = lax.broadcasted_iota(jnp.int32, (LW, LW), 1)
    source = ((row // 4) % 4) * 64 + (row // 16) * 4 + row % 4
    perm[...] = jnp.where(col == source, 1.0, 0.0).astype(BF16)
    clips = cf_row.shape[1]
    c_row = lax.broadcasted_iota(jnp.int32, (clips, clips), 0)
    c_col = lax.broadcasted_iota(jnp.int32, (clips, clips), 1)
    ends_col = jnp.sum(jnp.where(c_col <= c_row, cf_row[...], 0), axis=1, keepdims=True)
    ends_row = jnp.sum(jnp.where(c_row <= c_col, cf_col[...], 0), axis=0, keepdims=True)
    frame_lane = lax.broadcasted_iota(jnp.int32, (clips, LW), 1) // 4
    frame_sub = lax.broadcasted_iota(jnp.int32, (LW, clips), 0) // 4
    id_lane = jnp.sum(jnp.where(frame_lane >= ends_col, 1, 0), axis=0, keepdims=True)
    id_sub = jnp.sum(jnp.where(frame_sub >= ends_row, 1, 0), axis=1, keepdims=True)
    same = jnp.logical_and(id_lane == id_sub, row % 4 == col % 4)
    bias[...] = jnp.where(same, 0.0, NEGATIVE)

    masks = [head_mask(h) for h in range(HEADS_LOC)]

    loads[0].wait()
    for copy in ag_x:
        copy.wait_recv()
    x_all = xall[...].reshape(LW, D)
    for j in range(3):
        qkvs[j] = dot(x_all, ws[j]).astype(BF16)

    total = jnp.zeros((LW, LW), F32)
    for h in range(HEADS_LOC):
        p = softmax(dot_bt(qkvs[0] * masks[h], qkvs[1]) * HD ** (-0.5))
        probs[h] = p
        total = total + dot(p.astype(BF16), qkvs[2] * masks[h])
    attn = total.astype(BF16)
    attns[...] = attn.reshape(MP, ROWS, LW)

    loads[1].wait()
    for c in range(4):
        cols = pl.ds(c * 256, 256)
        rsend[0, :, :, cols] = dot(attn, wos[:, cols]).astype(BF16).reshape(MP, ROWS, 256)
    rs1 = scatter_mp(2, 0)
    own = dot(attns[m], wos[...])

    loads[2].wait()
    for copy in ag_g:
        copy.wait_recv()
    dat[...] = dot_bt(gall[...].reshape(LW, D), wot[...]).astype(BF16).reshape(MP, ROWS, LW)

    for copy in rs1:
        copy.wait_recv()
    hidden = x_ref[...].astype(F32) + own
    for k in range(3):
        hidden = hidden + rrecv[0, k].astype(F32)
    inv_h = lax.rsqrt(jnp.mean(hidden * hidden, -1, keepdims=True) + EPS)
    hid[...] = hidden
    nhall[m] = (hidden * inv_h).astype(BF16)
    ag_h = gather_mp(3, nhall.at[m], nhall)

    loads[3].wait()

    def exchange_block(which, block):
        def send(step, carry):
            to = block * 16 + lax.rem(f + step, 16)

            @pl.when(to != f)
            def _():
                remote(
                    a2send.at[which, to], a2recv.at[which, f],
                    a2_ssem.at[which], a2_rsem.at[which], to, m,
                ).start()

            return carry

        lax.fori_loop(0, 16, send, 0)

    def exchange_wait(which):
        some = pl.ds(0, FR - 1)
        return remote(
            a2send.at[which, some], a2recv.at[which, some],
            a2_ssem.at[which], a2_rsem.at[which], f, m,
        )

    def pack(which, block, parts):
        joined = jnp.concatenate(parts, axis=0)
        a2send[which, pl.ds(block * 16, 16)] = (
            dot(perm[...], joined).astype(BF16).reshape(16, 16, LW)
        )

    def unpack(which, target):
        for b in range(4):
            block = a2recv[which, 16 * b : 16 * b + 16].reshape(LW, LW)
            apart = dot_at(perm[...], block).astype(BF16)
            for t in range(4):
                target[t, 64 * b : 64 * b + 64] = apart[64 * t : 64 * t + 64]

    for at, k in enumerate((0, 1, 3, 2)):
        block = lax.rem(m + MP - k, MP)
        if k:
            ag_h[at - 1].wait_recv()
        rows = nhall[block]
        parts = [dot(rows, wt[j]).astype(BF16) for j in range(3)]
        pack(0, block, parts + [dat[block]])
        exchange_block(0, block)
    a2recv[0, f] = a2send[0, f]
    exchange_wait(0).wait_recv()
    unpack(0, tq)

    zero = jnp.zeros((LW, LW), F32)
    attn_t, d_q, d_k, d_v = zero, zero, zero, zero
    for h in range(HEADS_LOC):
        qm = tq[0] * masks[h]
        km = tq[1] * masks[h]
        vm = tq[2] * masks[h]
        om = tq[3] * masks[h]
        p = softmax(dot_bt(qm, tq[1]) * HD ** (-0.5) + bias[...])
        pb = p.astype(BF16)
        attn_t = attn_t + dot(pb, vm)
        d_v = d_v + dot_at(pb, om)
        ds = score_grads(p, dot_bt(om, tq[2]))
        d_q = d_q + dot(ds, km)
        d_k = d_k + dot_at(ds, qm)
    back = [t.astype(BF16) for t in (d_q, d_k, d_v, attn_t)]
    for b in range(4):
        pack(1, b, [t[64 * b : 64 * b + 64] for t in back])
    for b in range(4):
        exchange_block(1, lax.rem(f // 16 + b, 4))
    a2recv[1, f] = a2send[1, f]
    exchange_wait(1).wait_recv()
    unpack(1, dqkv)

    def project_back(which, grads, weights):
        for c in range(4):
            cols = pl.ds(c * 256, 256)
            part = dot_bt(grads[0], weights[0, cols])
            part = part + dot_bt(grads[1], weights[1, cols])
            part = part + dot_bt(grads[2], weights[2, cols])
            rsend[which, :, :, cols] = part.astype(BF16).reshape(MP, ROWS, 256)

    def own_back(grads_ref, weights):
        mine = pl.ds(pl.multiple_of(m * ROWS, ROWS), ROWS)
        part = dot_bt(grads_ref[0, mine], weights[0])
        part = part + dot_bt(grads_ref[1, mine], weights[1])
        return part + dot_bt(grads_ref[2, mine], weights[2])

    def weight_grad(which, j, left_ref, right):
        for c in range(4):
            left = left_ref[:, :, c * 256 : (c + 1) * 256].reshape(LW, 256)
            gbuf[which, j, 8 * c : 8 * c + 8] = (
                dot_at(left, right).astype(BF16).reshape(8, 2, 16, LW)
            )

    def core_send(which):
        copy = remote(
            gbuf.at[which, :, :, 1 - core], grecv1.at[which],
            c_send.at[which], c_recv.at[which], f + 1 - 2 * core, m,
        )
        copy.start()
        pending.append(copy)
        return copy

    def core_sum_x_send(which, copy):
        copy.wait_recv()
        for j in range(4):
            summed = gbuf[which, j, :, core].astype(F32) + grecv1[which, j].astype(F32)
            gsum1[which, j] = summed.astype(BF16).reshape(ZS, XS, 16, LW)
        copies = []
        for k in (1, 3, 2):
            to = lax.rem(xpos + k, XS)
            copy = remote(
                gsum1.at[which, :, :, to], grecv2.at[which, k - 1],
                x_send.at[which, k - 1], x_recv.at[which, k - 1],
                (zpos * XS + to) * 2 + core, m,
            )
            copy.start()
            copies.append(copy)
        pending.extend(copies)
        return copies

    def x_sum_z_send(which, copies):
        for copy in copies:
            copy.wait_recv()
        for j in range(4):
            summed = gsum1[which, j, :, xpos].astype(F32)
            for k in range(3):
                summed = summed + grecv2[which, k, j].astype(F32)
            gsum2[which, j] = summed.astype(BF16)
        copies = []
        for k in range(1, ZS):
            to = lax.rem(zpos + k, ZS)
            copy = remote(
                gsum2.at[which, :, to], grecv3.at[which, k - 1],
                z_send.at[which, k - 1], z_recv.at[which, k - 1],
                (to * XS + xpos) * 2 + core, m,
            )
            copy.start()
            copies.append(copy)
        pending.extend(copies)
        return copies

    def z_sum(which, copies, qkv_out, out_out):
        for copy in copies:
            copy.wait_recv()
        for j in range(4):
            summed = gsum2[which, j, zpos].astype(F32)
            for k in range(ZS - 1):
                summed = summed + grecv3[which, k, j].astype(F32)
            if j < 3:
                qkv_out[j] = summed
            else:
                out_out[...] = summed

    project_back(1, [dqkv[j] for j in range(3)], wt)
    rs2 = scatter_mp(4, 1)
    for j in range(3):
        weight_grad(0, j, nhall, dqkv[j])
    weight_grad(0, 3, gall, dqkv[3])
    core_t = core_send(0)
    d_nh = own_back(dqkv, wt)
    for copy in rs2:
        copy.wait_recv()
    for k in range(3):
        d_nh = d_nh + rrecv[1, k].astype(F32)
    hidden = hid[...]
    inv_h = lax.rsqrt(jnp.mean(hidden * hidden, -1, keepdims=True) + EPS)
    d_hidden = g_ref[...].astype(F32) + norm_back(hidden, inv_h, d_nh)
    dhid[...] = d_hidden
    dhall[m] = d_hidden.astype(BF16)
    ag_d = gather_mp(5, dhall.at[m], dhall)
    x_t = core_sum_x_send(0, core_t)
    for copy in ag_d:
        copy.wait_recv()

    das = dot_bt(dhall[...].reshape(LW, D), wos[...]).astype(BF16)
    d_q, d_k, d_v = zero, zero, zero
    for h in range(HEADS_LOC):
        om = das * masks[h]
        p = probs[h]
        d_v = d_v + dot_at(p.astype(BF16), om)
        ds = score_grads(p, dot_bt(om, qkvs[2]))
        d_q = d_q + dot(ds, qkvs[1] * masks[h])
        d_k = d_k + dot_at(ds, qkvs[0] * masks[h])
    grads_s = [t.astype(BF16) for t in (d_q, d_k, d_v)]
    for j in range(3):
        dqkv[4 + j] = grads_s[j]
        weight_grad(1, j, xall, grads_s[j])
    weight_grad(1, 3, dhall, attns[...].reshape(LW, LW))
    core_s = core_send(1)
    project_back(2, grads_s, ws)
    rs3 = scatter_mp(6, 2)
    z_t = x_sum_z_send(0, x_t)
    x_s = core_sum_x_send(1, core_s)
    d_nx = own_back(dqkv.at[4:7], ws)
    for copy in rs3:
        copy.wait_recv()
    for k in range(3):
        d_nx = d_nx + rrecv[2, k].astype(F32)
    x = x_ref[...].astype(F32)
    inv_x = lax.rsqrt(jnp.mean(x * x, -1, keepdims=True) + EPS)
    tok_ref[...] = (dhid[...] + norm_back(x, inv_x, d_nx)).astype(BF16)
    z_sum(0, z_t, gt_ref, gto_ref)
    z_s = x_sum_z_send(1, x_s)
    z_sum(1, z_s, gs_ref, gso_ref)
    for copy in pending:
        copy.wait_send()
    exchange_wait(0).wait_send()
    exchange_wait(1).wait_send()


def shards(x, g, ws, wos, wt, wot, clip_frames):
    clips = clip_frames.shape[0]
    vmem = pl.BlockSpec(memory_space=pltpu.VMEM)
    anywhere = pl.BlockSpec(memory_space=pl.ANY)
    dma = pltpu.SemaphoreType.DMA
    scratch = [
        pltpu.VMEM((3, D, LW), BF16),
        pltpu.VMEM((LW, D), BF16),
        pltpu.VMEM((3, D, LW), BF16),
        pltpu.VMEM((LW, D), BF16),
        pltpu.VMEM((MP, ROWS, D), BF16),
        pltpu.VMEM((MP, ROWS, D), BF16),
        pltpu.VMEM((MP, ROWS, D), BF16),
        pltpu.VMEM((MP, ROWS, D), BF16),
        pltpu.VMEM((LW, LW), BF16),
        pltpu.VMEM((LW, LW), F32),
        pltpu.VMEM((3, LW, LW), BF16),
        pltpu.VMEM((HEADS_LOC, LW, LW), F32),
        pltpu.VMEM((MP, ROWS, LW), BF16),
        pltpu.VMEM((MP, ROWS, LW), BF16),
        pltpu.VMEM((ROWS, D), F32),
        pltpu.VMEM((ROWS, D), F32),
        pltpu.VMEM((3, MP, ROWS, D), BF16),
        pltpu.VMEM((3, MP - 1, ROWS, D), BF16),
        pltpu.VMEM((2, FR, 16, LW), BF16),
        pltpu.VMEM((2, FR, 16, LW), BF16),
        pltpu.VMEM((4, LW, LW), BF16),
        pltpu.VMEM((7, LW, LW), BF16),
        pltpu.VMEM((2, 4, FR // 2, 2, 16, LW), BF16),
        pltpu.VMEM((2, 4, FR // 2, 16, LW), BF16),
        pltpu.VMEM((2, 4, ZS, XS, 16, LW), BF16),
        pltpu.VMEM((2, XS - 1, 4, ZS, 16, LW), BF16),
        pltpu.VMEM((2, 4, ZS, 16, LW), BF16),
        pltpu.VMEM((2, ZS - 1, 4, 16, LW), BF16),
        dma((4,)),
        dma((7, 3)),
        dma((7, 3)),
        dma((2,)),
        dma((2,)),
        dma((2,)),
        dma((2,)),
        dma((2, XS - 1)),
        dma((2, XS - 1)),
        dma((2, ZS - 1)),
        dma((2, ZS - 1)),
    ]
    tokens, gs, gso, gt, gto = pl.pallas_call(
        kernel,
        out_shape=(
            jax.ShapeDtypeStruct((ROWS, D), BF16),
            jax.ShapeDtypeStruct((3, 16, LW), F32),
            jax.ShapeDtypeStruct((16, LW), F32),
            jax.ShapeDtypeStruct((3, 16, LW), F32),
            jax.ShapeDtypeStruct((16, LW), F32),
        ),
        in_specs=[vmem] * 4 + [anywhere] * 4,
        out_specs=[vmem] * 5,
        scratch_shapes=scratch,
        compiler_params=pltpu.CompilerParams(
            collective_id=0, has_side_effects=True, vmem_limit_bytes=48 * 1024 * 1024
        ),
        cost_estimate=pl.CostEstimate(
            flops=3_500_000_000, bytes_accessed=6_000_000, transcendentals=1_000_000
        ),
    )(
        x.reshape(ROWS, D), g.reshape(ROWS, D),
        clip_frames.reshape(1, clips), clip_frames.reshape(clips, 1),
        ws, wos, wt, wot,
    )
    return tokens.reshape(1, ROWS, D), gs, gso.T, gt, gto.T


def solution(mesh):
    placed = (
        P("frames", "mp", None),
        P("frames", "mp", None),
        P(None, None, "mp"),
        P("mp", None),
        P(None, None, "mp"),
        P("mp", None),
        P(),
    )
    return jax.shard_map(
        shards,
        mesh=mesh,
        in_specs=placed,
        out_specs=(
            P("frames", "mp", None),
            P(None, "frames", "mp"),
            P("mp", "frames"),
            P(None, "frames", "mp"),
            P("mp", "frames"),
        ),
        check_vma=False,
    )
```

time: 724 us -> 133 us (0.18)
  waiting for transfers between devices: 507 us -> 0 us
  Pallas kernels: 0 us -> 119 us
  blocking collectives: 95.2 us -> 0 us
  matrix products: 40.6 us -> 0 us
  starting transfers between devices: 23.5 us -> 0 us
  local copies, waits for them, and re-layouts: 26.3 us -> 11.2 us
  other arithmetic: 14.7 us -> 0 us
  between operations: 15.3 us -> 0.65 us
    reduce_scatter x5 -> x0, waiting for transfers between devices: 303 us -> none  [the longest x1 142 us: shards(): lax.psum_scatter(grad_spatial_out, 'frames', scatter_dimension=1, tiled=T...]
    unnamed x7 -> x0, waiting for transfers between devices: 189 us -> none
    pallas_call x0 -> x1, Pallas kernels: none -> 119 us  [shards(): pl.pallas_call(kernel, out_shape=(jax.ShapeDtypeStruct((ROWS, D), BF16),...]
    all_gather x4 -> x0, blocking collectives: 53.5 us -> none  [patch_rows(): return lax.all_gather(tensor, 'mp', axis=1, tiled=True)]
    all_to_all x2 -> x0, blocking collectives: 41.7 us -> none  [from_owners(): lax.all_to_all(tensor, 'frames', split_axis=1, concat_axis=2, tiled=True)]
    dot_general x22 -> x0, matrix products: 39.1 us -> none  [the longest x2 5.31 us: attend_back(): jnp.einsum('bhlm,' + key_layout + '->' + layout, d_scores, keys_in, prefe...]
    all_to_all x2 -> x0, starting transfers between devices: 22.8 us -> none  [to_owners(): lax.all_to_all(tensor, 'frames', split_axis=2, concat_axis=1, tiled=True)]
    all_to_all x2 -> x0, waiting for transfers between devices: 15.1 us -> none  [to_owners(): lax.all_to_all(tensor, 'frames', split_axis=2, concat_axis=1, tiled=True)]
  transfers between devices with their start and end apart: 8 -> 0, of which waited for: 5 -> 0; matrix products, arithmetic and copies ran while one was open for 5% -> 0% of each run, Pallas kernels for 0% -> 0%
where the time goes in v1:
time: 133 us; the launch traced here: 131 us
  Pallas kernels  119 us (89%)
  local copies, waits for them, and re-layouts  11.2 us (8%)
    pallas_call x1, Pallas kernels, shards(): pl.pallas_call(kernel, out_shape=(jax.ShapeDtypeStruct((ROWS, D), BF16),...  119 us
    unnamed x19, local copies, waits for them, and re-layouts  10.5 us

profile of v1, /device:TPU:8, one launch (start us, length us, event | category | flops | bytes accessed | tf_op | source)
XLA Modules:
  0.0 130.9 jit_solution(17732407711814920820)
XLA Ops:
  0.6 0.7 copy.12.cf_col
  1.4 0.0 copy-start
  1.4 0.7 copy-done
  2.0 0.0 copy-start.1
  2.0 1.4 %copy-done.1 = bf16[3,1024,256]{2,1,0:T(8,128)(2,1)S(1)} copy-done((bf16[3,1024,256]{2,1,0:T(8,128)(2,1)S(1)}, bf16[3,1024,256]{2,1,0:T(8,128)(2,1)}, u32[]{:S(2)}) %copy-start.1) | copy-done | bytes 1572888
  3.4 0.0 copy-start.2
  3.4 1.4 %copy-done.2 = bf16[3,1024,256]{2,1,0:T(8,128)(2,1)S(1)} copy-done((bf16[3,1024,256]{2,1,0:T(8,128)(2,1)S(1)}, bf16[3,1024,256]{2,1,0:T(8,128)(2,1)}, u32[]{:S(2)}) %copy-start.2) | copy-done | bytes 1572888
  4.8 0.0 copy-start.3
  4.8 1.0 copy-done.3
  5.9 0.0 copy-start.4
  5.9 1.0 copy-done.4
  6.9 0.0 copy-start.5
  6.9 0.9 copy-done.5
  7.8 0.0 copy-start.6
  7.8 0.9 copy-done.6
  8.7 119.0 %shard_map.110 = (bf16[64,1024]{1,0:T(8,128)(2,1)S(1)}, f32[3,16,256]{2,1,0:T(8,128)S(1)}, f32[16,256]{1,0:T(8,128)S(1)}, f32[3,16,256]{2,1,0:T(8,128)S(1)}, f32[16,256]{1,0:T(8,128)S(1)}) custom-call(bf16[64,1024]{1,0:T(8,128)(2,1)S(1)} %bitcast.12, bf16[64,1024]{1,0:T(8,128)(2,1)S(1)} %bitcast.13, s32[1,32]{1,0:T(1,128)S(1)} %bitcast.11, ...), custom_call_target="tpu_custom_call" | custom-call | flops 3500000000 | bytes 6000000 | tf_op jit(solution)/shard_map/pallas_call | solution.py:447
  127.8 0.7 copy.18
  128.4 0.6 copy.19
  129.0 0.6 copy.20
  129.6 0.6 copy.21
  130.3 0.6 copy.22
Async XLA Ops:
  1.4 0.7 copy-start
  2.0 1.4 %copy-start.1 = (bf16[3,1024,256]{2,1,0:T(8,128)(2,1)S(1)}, bf16[3,1024,256]{2,1,0:T(8,128)(2,1)}, u32[]{:S(2)}) copy-start(bf16[3,1024,256]{2,1,0:T(8,128)(2,1)} %ws_hbm.1) | copy-start | bytes 4718596
  3.4 1.4 %copy-start.2 = (bf16[3,1024,256]{2,1,0:T(8,128)(2,1)S(1)}, bf16[3,1024,256]{2,1,0:T(8,128)(2,1)}, u32[]{:S(2)}) copy-start(bf16[3,1024,256]{2,1,0:T(8,128)(2,1)} %wt_hbm.1) | copy-start | bytes 4718596
  4.8 1.0 copy-start.3
  5.9 1.0 copy-start.4
  6.9 0.9 copy-start.5
  7.8 0.9 copy-start.6

commit v2 on v1

--- a/solution.py
+++ b/solution.py
@@ -12,6 +12,8 @@
 MP = 4
 XS = 4
 ZS = 8
+PL = 8
+HALO = 3
 D = 1024
 LW = 256
 ROWS = 64
@@ -54,19 +56,21 @@
 
 
 def kernel(
-    x_ref, g_ref, cf_row, cf_col, ws_hbm, wos_hbm, wt_hbm, wot_hbm,
+    x_hbm, g_hbm, cf_hbm, ws_hbm, wos_hbm, wt_hbm, wot_hbm,
     tok_ref, gs_ref, gso_ref, gt_ref, gto_ref,
-    ws, wos, wt, wot, xall, gall, nhall, dhall,
-    perm, bias, qkvs, probs, attns, dat, hid, dhid,
-    rsend, rrecv, a2send, a2recv, tq, dqkv,
+    x_ref, g_ref, cf_row, ws, wos, wt, wot, xall, gall, nhall, dhall,
+    bias, qkvs, probs, attns, hid, dhid,
+    rsend, rrecv, tsend, tbuf, tres, dqkv, dqs,
     gbuf, grecv1, gsum1, grecv2, gsum2, grecv3,
-    w_sem, mp_send, mp_recv, a2_ssem, a2_rsem, c_send, c_recv, x_send, x_recv, z_send, z_recv,
+    w_sem, mp_send, mp_recv, t_send, t_recv, h_send, h_recv, b_send, b_recv,
+    c_send, c_recv, x_send, x_recv, z_send, z_recv,
 ):
     f = lax.axis_index("frames")
     m = lax.axis_index("mp")
     core = lax.rem(f, 2)
     xpos = lax.rem(f // 2, XS)
-    zpos = f // (2 * XS)
+    zpos = f // PL
+    w = lax.rem(f, PL)
 
     def remote(src, dst, ssem, rsem, to_f, to_m):
         return pltpu.make_async_remote_copy(
@@ -79,7 +83,10 @@
     loads = [
         pltpu.make_async_copy(hbm, vmem, w_sem.at[i])
         for i, (hbm, vmem) in enumerate(
-            ((ws_hbm, ws), (wos_hbm, wos), (wot_hbm, wot), (wt_hbm, wt))
+            (
+                (x_hbm, x_ref), (g_hbm, g_ref), (cf_hbm, cf_row),
+                (ws_hbm, ws), (wos_hbm, wos), (wot_hbm, wot), (wt_hbm, wt),
+            )
         )
     ]
     for load in loads:
@@ -87,17 +94,18 @@
 
     barrier = pltpu.get_barrier_semaphore()
 
-    def greet(step, carry):
-        pl.semaphore_signal(
-            barrier, inc=1, device_id=(lax.rem(f + step, FR), m), device_id_type=MESH
-        )
-        return carry
-
     for k in range(1, MP):
         pl.semaphore_signal(
             barrier, inc=1, device_id=(f, lax.rem(m + k, MP)), device_id_type=MESH
         )
-    lax.fori_loop(1, FR, greet, 0)
+    for k in range(1, PL):
+        pl.semaphore_signal(
+            barrier, inc=1, device_id=(zpos * PL + lax.rem(w + k, PL), m), device_id_type=MESH
+        )
+    for k in range(1, ZS):
+        pl.semaphore_signal(
+            barrier, inc=1, device_id=(lax.rem(zpos + k, ZS) * PL + w, m), device_id_type=MESH
+        )
 
     def gather_mp(phase, src, buf):
         copies = []
@@ -124,36 +132,49 @@
         pending.extend(copies)
         return copies
 
+    loads[0].wait()
     x = x_ref[...].astype(F32)
     inv_x = lax.rsqrt(jnp.mean(x * x, -1, keepdims=True) + EPS)
     xall[m] = (x * inv_x).astype(BF16)
+    pl.semaphore_wait(barrier, MP - 1 + PL - 1 + ZS - 1)
+
+    ag_x = gather_mp(0, xall.at[m], xall)
+
+    loads[1].wait()
+    loads[2].wait()
     gall[m] = g_ref[...]
-    pl.semaphore_wait(barrier, FR - 1 + MP - 1)
-
-    ag_x = gather_mp(0, xall.at[m], xall)
-    ag_g = gather_mp(1, g_ref, gall)
-
     row = lax.broadcasted_iota(jnp.int32, (LW, LW), 0)
     col = lax.broadcasted_iota(jnp.int32, (LW, LW), 1)
-    source = ((row // 4) % 4) * 64 + (row // 16) * 4 + row % 4
-    perm[...] = jnp.where(col == source, 1.0, 0.0).astype(BF16)
     clips = cf_row.shape[1]
     c_row = lax.broadcasted_iota(jnp.int32, (clips, clips), 0)
     c_col = lax.broadcasted_iota(jnp.int32, (clips, clips), 1)
     ends_col = jnp.sum(jnp.where(c_col <= c_row, cf_row[...], 0), axis=1, keepdims=True)
-    ends_row = jnp.sum(jnp.where(c_row <= c_col, cf_col[...], 0), axis=0, keepdims=True)
-    frame_lane = lax.broadcasted_iota(jnp.int32, (clips, LW), 1) // 4
-    frame_sub = lax.broadcasted_iota(jnp.int32, (LW, clips), 0) // 4
-    id_lane = jnp.sum(jnp.where(frame_lane >= ends_col, 1, 0), axis=0, keepdims=True)
-    id_sub = jnp.sum(jnp.where(frame_sub >= ends_row, 1, 0), axis=1, keepdims=True)
-    same = jnp.logical_and(id_lane == id_sub, row % 4 == col % 4)
+    ends_row = jnp.sum(jnp.where(c_row == c_col, ends_col, 0), axis=0, keepdims=True)
+
+    def clip_of(slot, ends, axis):
+        frame = lax.rem(zpos * PL + FR - HALO + slot, FR)
+        count = jnp.sum(jnp.where(frame >= ends, 1, 0), axis=axis, keepdims=True)
+        return count
+
+    slot_lane = lax.broadcasted_iota(jnp.int32, (clips, LW), 1) // 16
+    slot_sub = lax.broadcasted_iota(jnp.int32, (LW, clips), 0) // 16
+    id_lane = clip_of(slot_lane, ends_col, 0)
+    id_sub = clip_of(slot_sub, ends_row, 1)
+    used = PL + 2 * HALO
+    id_lane = jnp.where(col[:1] // 16 < used, id_lane, -1)
+    id_sub = jnp.where(row[:, :1] // 16 < used, id_sub, -1)
+    same = jnp.logical_and(id_lane == id_sub, row % 16 == col % 16)
     bias[...] = jnp.where(same, 0.0, NEGATIVE)
+    for t in range(4):
+        for g in range(2):
+            tbuf[t, g, used:] = jnp.zeros((16 - used, 16, LW), BF16)
 
     masks = [head_mask(h) for h in range(HEADS_LOC)]
 
-    loads[0].wait()
+    loads[3].wait()
     for copy in ag_x:
         copy.wait_recv()
+    ag_g = gather_mp(1, g_ref, gall)
     x_all = xall[...].reshape(LW, D)
     for j in range(3):
         qkvs[j] = dot(x_all, ws[j]).astype(BF16)
@@ -166,17 +187,17 @@
     attn = total.astype(BF16)
     attns[...] = attn.reshape(MP, ROWS, LW)
 
-    loads[1].wait()
+    loads[4].wait()
     for c in range(4):
         cols = pl.ds(c * 256, 256)
         rsend[0, :, :, cols] = dot(attn, wos[:, cols]).astype(BF16).reshape(MP, ROWS, 256)
     rs1 = scatter_mp(2, 0)
     own = dot(attns[m], wos[...])
 
-    loads[2].wait()
+    loads[5].wait()
     for copy in ag_g:
         copy.wait_recv()
-    dat[...] = dot_bt(gall[...].reshape(LW, D), wot[...]).astype(BF16).reshape(MP, ROWS, LW)
+    tsend[3] = dot_bt(gall[...].reshape(LW, D), wot[...]).astype(BF16).reshape(2, PL, 16, LW)
 
     for copy in rs1:
         copy.wait_recv()
@@ -188,77 +209,87 @@
     nhall[m] = (hidden * inv_h).astype(BF16)
     ag_h = gather_mp(3, nhall.at[m], nhall)
 
-    loads[3].wait()
-
-    def exchange_block(which, block):
-        def send(step, carry):
-            to = block * 16 + lax.rem(f + step, 16)
-
-            @pl.when(to != f)
-            def _():
-                remote(
-                    a2send.at[which, to], a2recv.at[which, f],
-                    a2_ssem.at[which], a2_rsem.at[which], to, m,
-                ).start()
-
-            return carry
-
-        lax.fori_loop(0, 16, send, 0)
-
-    def exchange_wait(which):
-        some = pl.ds(0, FR - 1)
+    loads[6].wait()
+    for copy in ag_h:
+        copy.wait_recv()
+    h_all = nhall[...].reshape(LW, D)
+    for j in range(3):
+        tsend[j] = dot(h_all, wt[j]).astype(BF16).reshape(2, PL, 16, LW)
+
+    there = []
+    for g in range(2):
+        for k in range(1, PL):
+            to = lax.rem(w + k, PL)
+            copy = remote(
+                tsend.at[:, g, to], tbuf.at[:, g, HALO + w],
+                t_send.at[g, k - 1], t_recv.at[g, k - 1], zpos * PL + to, m,
+            )
+            copy.start()
+            there.append(copy)
+    pending.extend(there)
+    for t in range(4):
+        for g in range(2):
+            tbuf[t, g, HALO + w] = tsend[t, g, w]
+
+    def hand_on(g, frame):
+        def to_plane(step, slot):
+            return remote(
+                tbuf.at[:, g, HALO + frame], tbuf.at[:, g, slot],
+                h_send.at[g], h_recv.at[g], lax.rem(zpos + step, ZS) * PL + w, m,
+            )
+
+        @pl.when(frame < HALO)
+        def _():
+            to_plane(ZS - 1, HALO + PL + frame).start()
+
+        @pl.when(frame >= PL - HALO)
+        def _():
+            to_plane(1, frame - (PL - HALO)).start()
+
+    def hand_wait(g):
+        some = pl.ds(0, 2 * HALO)
         return remote(
-            a2send.at[which, some], a2recv.at[which, some],
-            a2_ssem.at[which], a2_rsem.at[which], f, m,
-        )
-
-    def pack(which, block, parts):
-        joined = jnp.concatenate(parts, axis=0)
-        a2send[which, pl.ds(block * 16, 16)] = (
-            dot(perm[...], joined).astype(BF16).reshape(16, 16, LW)
-        )
-
-    def unpack(which, target):
-        for b in range(4):
-            block = a2recv[which, 16 * b : 16 * b + 16].reshape(LW, LW)
-            apart = dot_at(perm[...], block).astype(BF16)
-            for t in range(4):
-                target[t, 64 * b : 64 * b + 64] = apart[64 * t : 64 * t + 64]
-
-    for at, k in enumerate((0, 1, 3, 2)):
-        block = lax.rem(m + MP - k, MP)
-        if k:
-            ag_h[at - 1].wait_recv()
-        rows = nhall[block]
-        parts = [dot(rows, wt[j]).astype(BF16) for j in range(3)]
-        pack(0, block, parts + [dat[block]])
-        exchange_block(0, block)
-    a2recv[0, f] = a2send[0, f]
-    exchange_wait(0).wait_recv()
-    unpack(0, tq)
+            tbuf.at[:, g, some], tbuf.at[:, g, some], h_send.at[g], h_recv.at[g], f, m
+        )
+
+    for g in range(2):
+        hand_on(g, w)
+        for k in range(1, PL):
+            there[g * (PL - 1) + k - 1].wait_recv()
+            hand_on(g, lax.rem(w + PL - k, PL))
 
     zero = jnp.zeros((LW, LW), F32)
-    attn_t, d_q, d_k, d_v = zero, zero, zero, zero
-    for h in range(HEADS_LOC):
-        qm = tq[0] * masks[h]
-        km = tq[1] * masks[h]
-        vm = tq[2] * masks[h]
-        om = tq[3] * masks[h]
-        p = softmax(dot_bt(qm, tq[1]) * HD ** (-0.5) + bias[...])
-        pb = p.astype(BF16)
-        attn_t = attn_t + dot(pb, vm)
-        d_v = d_v + dot_at(pb, om)
-        ds = score_grads(p, dot_bt(om, tq[2]))
-        d_q = d_q + dot(ds, km)
-        d_k = d_k + dot_at(ds, qm)
-    back = [t.astype(BF16) for t in (d_q, d_k, d_v, attn_t)]
-    for b in range(4):
-        pack(1, b, [t[64 * b : 64 * b + 64] for t in back])
-    for b in range(4):
-        exchange_block(1, lax.rem(f // 16 + b, 4))
-    a2recv[1, f] = a2send[1, f]
-    exchange_wait(1).wait_recv()
-    unpack(1, dqkv)
+    back = []
+    for g in range(2):
+        hand_wait(g).wait_recv()
+        queries, keys, values, upstream = [tbuf[t, g].reshape(LW, LW) for t in range(4)]
+        attn_t, d_q, d_k, d_v = zero, zero, zero, zero
+        for h in range(HEADS_LOC):
+            qm = queries * masks[h]
+            om = upstream * masks[h]
+            p = softmax(dot_bt(qm, keys) * HD ** (-0.5) + bias[...])
+            pb = p.astype(BF16)
+            attn_t = attn_t + dot(pb, values * masks[h])
+            d_v = d_v + dot_at(pb, om)
+            ds = score_grads(p, dot_bt(om, values))
+            d_q = d_q + dot(ds, keys * masks[h])
+            d_k = d_k + dot_at(ds, qm)
+        for t, full in enumerate((d_q, d_k, d_v, attn_t)):
+            mine = full[16 * HALO : 16 * (HALO + PL)]
+            tres[t, g] = mine.astype(BF16).reshape(PL, 16, LW)
+        for k in range(1, PL):
+            to = lax.rem(w + k, PL)
+            copy = remote(
+                tres.at[:, g, to], dqkv.at[:, g, w],
+                b_send.at[g, k - 1], b_recv.at[g, k - 1], zpos * PL + to, m,
+            )
+            copy.start()
+            back.append(copy)
+        for t in range(4):
+            dqkv[t, g, w] = tres[t, g, w]
+    pending.extend(back)
+    for copy in back:
+        copy.wait_recv()
 
     def project_back(which, grads, weights):
         for c in range(4):
@@ -268,11 +299,10 @@
             part = part + dot_bt(grads[2], weights[2, cols])
             rsend[which, :, :, cols] = part.astype(BF16).reshape(MP, ROWS, 256)
 
-    def own_back(grads_ref, weights):
-        mine = pl.ds(pl.multiple_of(m * ROWS, ROWS), ROWS)
-        part = dot_bt(grads_ref[0, mine], weights[0])
-        part = part + dot_bt(grads_ref[1, mine], weights[1])
-        return part + dot_bt(grads_ref[2, mine], weights[2])
+    def own_back(grads, weights):
+        part = dot_bt(grads[0], weights[0])
+        part = part + dot_bt(grads[1], weights[1])
+        return part + dot_bt(grads[2], weights[2])
 
     def weight_grad(which, j, left_ref, right):
         for c in range(4):
@@ -341,13 +371,15 @@
             else:
                 out_out[...] = summed
 
-    project_back(1, [dqkv[j] for j in range(3)], wt)
+    grads_t = [dqkv[j].reshape(LW, LW) for j in range(4)]
+    project_back(1, grads_t[:3], wt)
     rs2 = scatter_mp(4, 1)
     for j in range(3):
-        weight_grad(0, j, nhall, dqkv[j])
-    weight_grad(0, 3, gall, dqkv[3])
+        weight_grad(0, j, nhall, grads_t[j])
+    weight_grad(0, 3, gall, grads_t[3])
     core_t = core_send(0)
-    d_nh = own_back(dqkv, wt)
+    half = pl.ds(4 * lax.rem(m, 2), 4)
+    d_nh = own_back([dqkv[j, m // 2, half].reshape(ROWS, LW) for j in range(3)], wt)
     for copy in rs2:
         copy.wait_recv()
     for k in range(3):
@@ -373,7 +405,7 @@
         d_k = d_k + dot_at(ds, qkvs[0] * masks[h])
     grads_s = [t.astype(BF16) for t in (d_q, d_k, d_v)]
     for j in range(3):
-        dqkv[4 + j] = grads_s[j]
+        dqs[j] = grads_s[j].reshape(MP, ROWS, LW)
         weight_grad(1, j, xall, grads_s[j])
     weight_grad(1, 3, dhall, attns[...].reshape(LW, LW))
     core_s = core_send(1)
@@ -381,7 +413,7 @@
     rs3 = scatter_mp(6, 2)
     z_t = x_sum_z_send(0, x_t)
     x_s = core_sum_x_send(1, core_s)
-    d_nx = own_back(dqkv.at[4:7], ws)
+    d_nx = own_back([dqs[j, m] for j in range(3)], ws)
     for copy in rs3:
         copy.wait_recv()
     for k in range(3):
@@ -394,16 +426,18 @@
     z_sum(1, z_s, gs_ref, gso_ref)
     for copy in pending:
         copy.wait_send()
-    exchange_wait(0).wait_send()
-    exchange_wait(1).wait_send()
+    for g in range(2):
+        hand_wait(g).wait_send()
 
 
 def shards(x, g, ws, wos, wt, wot, clip_frames):
     clips = clip_frames.shape[0]
     vmem = pl.BlockSpec(memory_space=pltpu.VMEM)
-    anywhere = pl.BlockSpec(memory_space=pl.ANY)
     dma = pltpu.SemaphoreType.DMA
     scratch = [
+        pltpu.VMEM((ROWS, D), BF16),
+        pltpu.VMEM((ROWS, D), BF16),
+        pltpu.VMEM((1, clips), jnp.int32),
         pltpu.VMEM((3, D, LW), BF16),
         pltpu.VMEM((LW, D), BF16),
         pltpu.VMEM((3, D, LW), BF16),
@@ -412,31 +446,34 @@
         pltpu.VMEM((MP, ROWS, D), BF16),
         pltpu.VMEM((MP, ROWS, D), BF16),
         pltpu.VMEM((MP, ROWS, D), BF16),
-        pltpu.VMEM((LW, LW), BF16),
         pltpu.VMEM((LW, LW), F32),
         pltpu.VMEM((3, LW, LW), BF16),
         pltpu.VMEM((HEADS_LOC, LW, LW), F32),
-        pltpu.VMEM((MP, ROWS, LW), BF16),
         pltpu.VMEM((MP, ROWS, LW), BF16),
         pltpu.VMEM((ROWS, D), F32),
         pltpu.VMEM((ROWS, D), F32),
         pltpu.VMEM((3, MP, ROWS, D), BF16),
         pltpu.VMEM((3, MP - 1, ROWS, D), BF16),
-        pltpu.VMEM((2, FR, 16, LW), BF16),
-        pltpu.VMEM((2, FR, 16, LW), BF16),
-        pltpu.VMEM((4, LW, LW), BF16),
-        pltpu.VMEM((7, LW, LW), BF16),
+        pltpu.VMEM((4, 2, PL, 16, LW), BF16),
+        pltpu.VMEM((4, 2, 16, 16, LW), BF16),
+        pltpu.VMEM((4, 2, PL, 16, LW), BF16),
+        pltpu.VMEM((4, 2, PL, 16, LW), BF16),
+        pltpu.VMEM((3, MP, ROWS, LW), BF16),
         pltpu.VMEM((2, 4, FR // 2, 2, 16, LW), BF16),
         pltpu.VMEM((2, 4, FR // 2, 16, LW), BF16),
         pltpu.VMEM((2, 4, ZS, XS, 16, LW), BF16),
         pltpu.VMEM((2, XS - 1, 4, ZS, 16, LW), BF16),
         pltpu.VMEM((2, 4, ZS, 16, LW), BF16),
         pltpu.VMEM((2, ZS - 1, 4, 16, LW), BF16),
-        dma((4,)),
+        dma((7,)),
         dma((7, 3)),
         dma((7, 3)),
+        dma((2, PL - 1)),
+        dma((2, PL - 1)),
         dma((2,)),
         dma((2,)),
+        dma((2, PL - 1)),
+        dma((2, PL - 1)),
         dma((2,)),
         dma((2,)),
         dma((2, XS - 1)),
@@ -453,19 +490,17 @@
             jax.ShapeDtypeStruct((3, 16, LW), F32),
             jax.ShapeDtypeStruct((16, LW), F32),
         ),
-        in_specs=[vmem] * 4 + [anywhere] * 4,
+        in_specs=[pl.BlockSpec(memory_space=pltpu.HBM)] * 7,
         out_specs=[vmem] * 5,
         scratch_shapes=scratch,
         compiler_params=pltpu.CompilerParams(
-            collective_id=0, has_side_effects=True, vmem_limit_bytes=48 * 1024 * 1024
+            collective_id=0, has_side_effects=True, vmem_limit_bytes=60 * 1024 * 1024
         ),
         cost_estimate=pl.CostEstimate(
             flops=3_500_000_000, bytes_accessed=6_000_000, transcendentals=1_000_000
         ),
     )(
-        x.reshape(ROWS, D), g.reshape(ROWS, D),
-        clip_frames.reshape(1, clips), clip_frames.reshape(clips, 1),
-        ws, wos, wt, wot,
+        x.reshape(ROWS, D), g.reshape(ROWS, D), clip_frames.reshape(1, clips), ws, wos, wt, wot,
     )
     return tokens.reshape(1, ROWS, D), gs, gso.T, gt, gto.T
 

time: 133 us -> 111 us (0.83); the launches traced: 131 us -> 110 us
  Pallas kernels: 119 us -> 103 us
  local copies, waits for them, and re-layouts: 11.2 us -> 7.05 us
    pallas_call x1, Pallas kernels: 119 us -> 103 us  [shards(): pl.pallas_call(kernel, out_shape=(jax.ShapeDtypeStruct((ROWS, D), BF16),...]
    unnamed x19 -> x5, local copies, waits for them, and re-layouts: 10.5 us -> 7.05 us
where the time goes in v2:
time: 111 us; the launch traced here: 110 us
  Pallas kernels  103 us (93%)
  local copies, waits for them, and re-layouts  7.05 us (6%)
    pallas_call x1, Pallas kernels, shards(): pl.pallas_call(kernel, out_shape=(jax.ShapeDtypeStruct((ROWS, D), BF16),...  103 us
    unnamed x5, local copies, waits for them, and re-layouts  7.05 us

profile of v2, /device:TPU:8, one launch (start us, length us, event | category | flops | bytes accessed | tf_op | source)
XLA Modules:
  0.0 110.5 jit_solution(13623053551327980877)
XLA Ops:
  0.6 102.8 %shard_map.110 = (bf16[64,1024]{1,0:T(8,128)(2,1)}, f32[3,16,256]{2,1,0:T(8,128)}, f32[16,256]{1,0:T(8,128)}, f32[3,16,256]{2,1,0:T(8,128)}, f32[16,256]{1,0:T(8,128)}) custom-call(bf16[64,1024]{1,0:T(8,128)(2,1)} %bitcast.9, bf16[64,1024]{1,0:T(8,128)(2,1)} %bitcast.10, s32[1,32]{1,0:T(1,128)} %bitcast.11, bf16[3,1024,256]{2,1,0:T(8,128)(2,1)} %ws_hbm.1, ...), custom_call_target="tpu_custom_call" | custom-call | flops 3500000000 | bytes 6000000 | tf_op jit(solution)/shard_map/pallas_call | solution.py:484
  103.4 1.6 %copy.17 = bf16[1,64,1024]{2,1,0:T(8,128)(2,1)} copy(bf16[1,64,1024]{2,1,0:T(8,128)(2,1)} %bitcast.6) | data formatting | bytes 262144
  105.0 1.4 %copy.18 = f32[3,16,256]{2,1,0:T(8,128)} copy(f32[3,16,256]{2,1,0:T(8,128)} %get-tuple-element.21) | data formatting | bytes 98304
  106.4 1.3 %copy.19 = f32[256,16]{0,1:T(8,128)} copy(f32[256,16]{0,1:T(8,128)} %bitcast.8) | data formatting | bytes 32768
  107.7 1.4 %copy.20 = f32[3,16,256]{2,1,0:T(8,128)} copy(f32[3,16,256]{2,1,0:T(8,128)} %get-tuple-element.23) | data formatting | bytes 98304
  109.1 1.3 %copy.21 = f32[256,16]{0,1:T(8,128)} copy(f32[256,16]{0,1:T(8,128)} %bitcast.7) | data formatting | bytes 32768

commit v3 on v2

--- a/solution.py
+++ b/solution.py
@@ -304,33 +304,36 @@
         part = part + dot_bt(grads[1], weights[1])
         return part + dot_bt(grads[2], weights[2])
 
-    def weight_grad(which, j, left_ref, right):
+    def weight_grad(j, left_ref, right):
         for c in range(4):
             left = left_ref[:, :, c * 256 : (c + 1) * 256].reshape(LW, 256)
-            gbuf[which, j, 8 * c : 8 * c + 8] = (
-                dot_at(left, right).astype(BF16).reshape(8, 2, 16, LW)
-            )
-
-    def core_send(which):
+            gbuf[j, 8 * c : 8 * c + 8] = dot_at(left, right).astype(BF16).reshape(8, 2, 16, LW)
+
+    first = [0, 4, 5, 6, 7]
+    count = [4, 1, 1, 1, 1]
+
+    def core_send(b):
+        some = slice(first[b], first[b] + count[b])
         copy = remote(
-            gbuf.at[which, :, :, 1 - core], grecv1.at[which],
-            c_send.at[which], c_recv.at[which], f + 1 - 2 * core, m,
+            gbuf.at[some, :, 1 - core], grecv1.at[some],
+            c_send.at[b], c_recv.at[b], f + 1 - 2 * core, m,
         )
         copy.start()
         pending.append(copy)
         return copy
 
-    def core_sum_x_send(which, copy):
-        copy.wait_recv()
-        for j in range(4):
-            summed = gbuf[which, j, :, core].astype(F32) + grecv1[which, j].astype(F32)
-            gsum1[which, j] = summed.astype(BF16).reshape(ZS, XS, 16, LW)
+    def core_sum_x_send(b, copy):
+        copy.wait_recv()
+        some = slice(first[b], first[b] + count[b])
+        for j in range(some.start, some.stop):
+            summed = gbuf[j, :, core].astype(F32) + grecv1[j].astype(F32)
+            gsum1[j] = summed.astype(BF16).reshape(ZS, XS, 16, LW)
         copies = []
         for k in (1, 3, 2):
             to = lax.rem(xpos + k, XS)
             copy = remote(
-                gsum1.at[which, :, :, to], grecv2.at[which, k - 1],
-                x_send.at[which, k - 1], x_recv.at[which, k - 1],
+                gsum1.at[some, :, to], grecv2.at[k - 1, some],
+                x_send.at[b, k - 1], x_recv.at[b, k - 1],
                 (zpos * XS + to) * 2 + core, m,
             )
             copy.start()
@@ -338,20 +341,21 @@
         pending.extend(copies)
         return copies
 
-    def x_sum_z_send(which, copies):
+    def x_sum_z_send(b, copies):
         for copy in copies:
             copy.wait_recv()
-        for j in range(4):
-            summed = gsum1[which, j, :, xpos].astype(F32)
+        some = slice(first[b], first[b] + count[b])
+        for j in range(some.start, some.stop):
+            summed = gsum1[j, :, xpos].astype(F32)
             for k in range(3):
-                summed = summed + grecv2[which, k, j].astype(F32)
-            gsum2[which, j] = summed.astype(BF16)
+                summed = summed + grecv2[k, j].astype(F32)
+            gsum2[j] = summed.astype(BF16)
         copies = []
-        for k in range(1, ZS):
+        for k in (4, 3, 5, 2, 6, 1, 7):
             to = lax.rem(zpos + k, ZS)
             copy = remote(
-                gsum2.at[which, :, to], grecv3.at[which, k - 1],
-                z_send.at[which, k - 1], z_recv.at[which, k - 1],
+                gsum2.at[some, to], grecv3.at[k - 1, some],
+                z_send.at[b, k - 1], z_recv.at[b, k - 1],
                 (to * XS + xpos) * 2 + core, m,
             )
             copy.start()
@@ -359,24 +363,22 @@
         pending.extend(copies)
         return copies
 
-    def z_sum(which, copies, qkv_out, out_out):
+    def z_sum(b, copies, outs):
         for copy in copies:
             copy.wait_recv()
-        for j in range(4):
-            summed = gsum2[which, j, zpos].astype(F32)
+        for at, out in enumerate(outs):
+            j = first[b] + at
+            summed = gsum2[j, zpos].astype(F32)
             for k in range(ZS - 1):
-                summed = summed + grecv3[which, k, j].astype(F32)
-            if j < 3:
-                qkv_out[j] = summed
-            else:
-                out_out[...] = summed
+                summed = summed + grecv3[k, j].astype(F32)
+            out[...] = summed
 
     grads_t = [dqkv[j].reshape(LW, LW) for j in range(4)]
     project_back(1, grads_t[:3], wt)
     rs2 = scatter_mp(4, 1)
     for j in range(3):
-        weight_grad(0, j, nhall, grads_t[j])
-    weight_grad(0, 3, gall, grads_t[3])
+        weight_grad(j, nhall, grads_t[j])
+    weight_grad(3, gall, grads_t[3])
     core_t = core_send(0)
     half = pl.ds(4 * lax.rem(m, 2), 4)
     d_nh = own_back([dqkv[j, m // 2, half].reshape(ROWS, LW) for j in range(3)], wt)
@@ -394,26 +396,38 @@
     for copy in ag_d:
         copy.wait_recv()
 
+    weight_grad(7, dhall, attns[...].reshape(LW, LW))
+    core_o = core_send(4)
     das = dot_bt(dhall[...].reshape(LW, D), wos[...]).astype(BF16)
-    d_q, d_k, d_v = zero, zero, zero
+
+    def keep(j, grad):
+        dqs[j] = grad.astype(BF16).reshape(MP, ROWS, LW)
+        weight_grad(4 + j, xall, dqs[j].reshape(LW, LW))
+        return core_send(1 + j)
+
+    d_v = zero
     for h in range(HEADS_LOC):
-        om = das * masks[h]
-        p = probs[h]
-        d_v = d_v + dot_at(p.astype(BF16), om)
-        ds = score_grads(p, dot_bt(om, qkvs[2]))
+        d_v = d_v + dot_at(probs[h].astype(BF16), das * masks[h])
+    core_v = keep(2, d_v)
+    x_o = core_sum_x_send(4, core_o)
+    d_q, d_k = zero, zero
+    for h in range(HEADS_LOC):
+        ds = score_grads(probs[h], dot_bt(das * masks[h], qkvs[2]))
         d_q = d_q + dot(ds, qkvs[1] * masks[h])
         d_k = d_k + dot_at(ds, qkvs[0] * masks[h])
-    grads_s = [t.astype(BF16) for t in (d_q, d_k, d_v)]
-    for j in range(3):
-        dqs[j] = grads_s[j].reshape(MP, ROWS, LW)
-        weight_grad(1, j, xall, grads_s[j])
-    weight_grad(1, 3, dhall, attns[...].reshape(LW, LW))
-    core_s = core_send(1)
-    project_back(2, grads_s, ws)
+    core_q = keep(0, d_q)
+    core_k = keep(1, d_k)
+    x_v = core_sum_x_send(3, core_v)
+    z_t = x_sum_z_send(0, x_t)
+    x_q = core_sum_x_send(1, core_q)
+    x_k = core_sum_x_send(2, core_k)
+    project_back(2, [dqs[j].reshape(LW, LW) for j in range(3)], ws)
     rs3 = scatter_mp(6, 2)
-    z_t = x_sum_z_send(0, x_t)
-    x_s = core_sum_x_send(1, core_s)
+    z_o = x_sum_z_send(4, x_o)
+    z_v = x_sum_z_send(3, x_v)
+    z_sum(0, z_t, [gt_ref.at[0], gt_ref.at[1], gt_ref.at[2], gto_ref])
     d_nx = own_back([dqs[j, m] for j in range(3)], ws)
+    z_q = x_sum_z_send(1, x_q)
     for copy in rs3:
         copy.wait_recv()
     for k in range(3):
@@ -421,13 +435,20 @@
     x = x_ref[...].astype(F32)
     inv_x = lax.rsqrt(jnp.mean(x * x, -1, keepdims=True) + EPS)
     tok_ref[...] = (dhid[...] + norm_back(x, inv_x, d_nx)).astype(BF16)
-    z_sum(0, z_t, gt_ref, gto_ref)
-    z_s = x_sum_z_send(1, x_s)
-    z_sum(1, z_s, gs_ref, gso_ref)
+    z_k = x_sum_z_send(2, x_k)
+    z_sum(4, z_o, [gso_ref])
+    z_sum(3, z_v, [gs_ref.at[2]])
+    z_sum(1, z_q, [gs_ref.at[0]])
+    z_sum(2, z_k, [gs_ref.at[1]])
     for copy in pending:
         copy.wait_send()
     for g in range(2):
         hand_wait(g).wait_send()
+
+
+def deliver(*refs):
+    for source, target in zip(refs[:5], refs[5:]):
+        target[...] = source[...]
 
 
 def shards(x, g, ws, wos, wt, wot, clip_frames):
@@ -459,12 +480,12 @@
         pltpu.VMEM((4, 2, PL, 16, LW), BF16),
         pltpu.VMEM((4, 2, PL, 16, LW), BF16),
         pltpu.VMEM((3, MP, ROWS, LW), BF16),
-        pltpu.VMEM((2, 4, FR // 2, 2, 16, LW), BF16),
-        pltpu.VMEM((2, 4, FR // 2, 16, LW), BF16),
-        pltpu.VMEM((2, 4, ZS, XS, 16, LW), BF16),
-        pltpu.VMEM((2, XS - 1, 4, ZS, 16, LW), BF16),
-        pltpu.VMEM((2, 4, ZS, 16, LW), BF16),
-        pltpu.VMEM((2, ZS - 1, 4, 16, LW), BF16),
+        pltpu.VMEM((8, FR // 2, 2, 16, LW), BF16),
+        pltpu.VMEM((8, FR // 2, 16, LW), BF16),
+        pltpu.VMEM((8, ZS, XS, 16, LW), BF16),
+        pltpu.VMEM((XS - 1, 8, ZS, 16, LW), BF16),
+        pltpu.VMEM((8, ZS, 16, LW), BF16),
+        pltpu.VMEM((ZS - 1, 8, 16, LW), BF16),
         dma((7,)),
         dma((7, 3)),
         dma((7, 3)),
@@ -474,12 +495,12 @@
         dma((2,)),
         dma((2, PL - 1)),
         dma((2, PL - 1)),
-        dma((2,)),
-        dma((2,)),
-        dma((2, XS - 1)),
-        dma((2, XS - 1)),
-        dma((2, ZS - 1)),
-        dma((2, ZS - 1)),
+        dma((5,)),
+        dma((5,)),
+        dma((5, XS - 1)),
+        dma((5, XS - 1)),
+        dma((5, ZS - 1)),
+        dma((5, ZS - 1)),
     ]
     tokens, gs, gso, gt, gto = pl.pallas_call(
         kernel,
@@ -502,6 +523,14 @@
     )(
         x.reshape(ROWS, D), g.reshape(ROWS, D), clip_frames.reshape(1, clips), ws, wos, wt, wot,
     )
+    results = (tokens, gs, gso, gt, gto)
+    tokens, gs, gso, gt, gto = pl.pallas_call(
+        deliver,
+        out_shape=tuple(jax.ShapeDtypeStruct(r.shape, r.dtype) for r in results),
+        in_specs=[vmem] * 5,
+        out_specs=[vmem] * 5,
+        compiler_params=pltpu.CompilerParams(vmem_limit_bytes=60 * 1024 * 1024),
+    )(*results)
     return tokens.reshape(1, ROWS, D), gs, gso.T, gt, gto.T
 
 

time: 111 us -> 101 us (0.910); the launches traced: 110 us -> 99 us
  local copies, waits for them, and re-layouts: 7.05 us -> 0 us
  Pallas kernels: 103 us -> 98.4 us
    unnamed x5 -> x0, local copies, waits for them, and re-layouts: 7.05 us -> none
    pallas_call x1, Pallas kernels: 103 us -> 96.7 us  [shards(): pl.pallas_call(kernel, out_shape=(jax.ShapeDtypeStruct((ROWS, D), BF16),...]
    pallas_call x0 -> x1, Pallas kernels: none -> 1.66 us  [shards(): pl.pallas_call(deliver, out_shape=tuple((jax.ShapeDtypeStruct(r.shape, r....]
where the time goes in v3:
time: 101 us; the launch traced here: 99 us
  Pallas kernels  98.4 us (97%)
    pallas_call x1, Pallas kernels, shards(): pl.pallas_call(kernel, out_shape=(jax.ShapeDtypeStruct((ROWS, D), BF16),...  96.7 us

profile of v3, /device:TPU:8, one launch (start us, length us, event | category | flops | bytes accessed | tf_op | source)
XLA Modules:
  0.0 99.0 jit_solution(5916082682582043200)
XLA Ops:
  0.6 96.7 %shard_map.110 = (bf16[64,1024]{1,0:T(8,128)(2,1)}, f32[3,16,256]{2,1,0:T(8,128)}, f32[16,256]{1,0:T(8,128)}, f32[3,16,256]{2,1,0:T(8,128)}, f32[16,256]{1,0:T(8,128)}) custom-call(bf16[64,1024]{1,0:T(8,128)(2,1)} %bitcast.6, bf16[64,1024]{1,0:T(8,128)(2,1)} %bitcast.7, s32[1,32]{1,0:T(1,128)} %bitcast.11, bf16[3,1024,256]{2,1,0:T(8,128)(2,1)} %ws_hbm.1, ...), custom_call_target="tpu_custom_call" | custom-call | flops 3500000000 | bytes 6000000 | tf_op jit(solution)/shard_map/pallas_call | solution.py:505
  97.4 1.7 %shard_map.111 = (bf16[64,1024]{1,0:T(8,128)(2,1)}, f32[3,16,256]{2,1,0:T(8,128)}, f32[16,256]{1,0:T(8,128)}, f32[3,16,256]{2,1,0:T(8,128)}, f32[16,256]{1,0:T(8,128)}) custom-call(bf16[64,1024]{1,0:T(8,128)(2,1)} %get-tuple-element.15.refs_0_, f32[3,16,256]{2,1,0:T(8,128)} %get-tuple-element.16.refs_1_, f32[16,256]{1,0:T(8,128)} %get-tuple-element.17.refs_2_, ...), custom_call_target="tpu_custom_call" | custom-call | tf_op jit(solution)/shard_map/pallas_call | solution.py:527

commit v4 on v3

--- a/solution.py
+++ b/solution.py
@@ -107,11 +107,11 @@
             barrier, inc=1, device_id=(lax.rem(zpos + k, ZS) * PL + w, m), device_id_type=MESH
         )
 
-    def gather_mp(phase, src, buf):
+    def gather_mp(phase, src, buf, rows=slice(0, ROWS)):
         copies = []
         for k in (1, 3, 2):
             copy = remote(
-                src, buf.at[m], mp_send.at[phase, k - 1], mp_recv.at[phase, k - 1],
+                src.at[rows], buf.at[m, rows], mp_send.at[phase, k - 1], mp_recv.at[phase, k - 1],
                 f, lax.rem(m + k, MP),
             )
             copy.start()
@@ -174,7 +174,7 @@
     loads[3].wait()
     for copy in ag_x:
         copy.wait_recv()
-    ag_g = gather_mp(1, g_ref, gall)
+    ag_g = gather_mp(1, g_ref, gall, slice(0, ROWS // 2))
     x_all = xall[...].reshape(LW, D)
     for j in range(3):
         qkvs[j] = dot(x_all, ws[j]).astype(BF16)
@@ -192,12 +192,8 @@
         cols = pl.ds(c * 256, 256)
         rsend[0, :, :, cols] = dot(attn, wos[:, cols]).astype(BF16).reshape(MP, ROWS, 256)
     rs1 = scatter_mp(2, 0)
+    ag_g = ag_g + gather_mp(7, g_ref, gall, slice(ROWS // 2, ROWS))
     own = dot(attns[m], wos[...])
-
-    loads[5].wait()
-    for copy in ag_g:
-        copy.wait_recv()
-    tsend[3] = dot_bt(gall[...].reshape(LW, D), wot[...]).astype(BF16).reshape(2, PL, 16, LW)
 
     for copy in rs1:
         copy.wait_recv()
@@ -209,6 +205,57 @@
     nhall[m] = (hidden * inv_h).astype(BF16)
     ag_h = gather_mp(3, nhall.at[m], nhall)
 
+    def plane_send(part, source, target, ssems, rsems):
+        copies = []
+        for k in range(1, PL):
+            to = lax.rem(w + k, PL)
+            copy = remote(
+                source(to), target, ssems.at[part, k - 1], rsems.at[part, k - 1],
+                zpos * PL + to, m,
+            )
+            copy.start()
+            copies.append(copy)
+        pending.extend(copies)
+        return copies
+
+    def halo_view(part, slots):
+        return tbuf.at[3, :, slots] if part == 2 else tbuf.at[:3, part, slots]
+
+    def hand_on(part, frame):
+        def to_plane(step, slot):
+            return remote(
+                halo_view(part, HALO + frame), halo_view(part, slot),
+                h_send.at[part], h_recv.at[part], lax.rem(zpos + step, ZS) * PL + w, m,
+            )
+
+        @pl.when(frame < HALO)
+        def _():
+            to_plane(ZS - 1, HALO + PL + frame).start()
+
+        @pl.when(frame >= PL - HALO)
+        def _():
+            to_plane(1, frame - (PL - HALO)).start()
+
+    def hand_wait(part):
+        some = halo_view(part, pl.ds(0, 2 * HALO))
+        return remote(some, some, h_send.at[part], h_recv.at[part], f, m)
+
+    def receive(part, copies):
+        hand_on(part, w)
+        for k in range(1, PL):
+            copies[k - 1].wait_recv()
+            hand_on(part, lax.rem(w + PL - k, PL))
+
+    loads[5].wait()
+    for copy in ag_g:
+        copy.wait_recv()
+    tsend[3] = dot_bt(gall[...].reshape(LW, D), wot[...]).astype(BF16).reshape(2, PL, 16, LW)
+    there_up = plane_send(
+        2, lambda to: tsend.at[3, :, to], halo_view(2, HALO + w), t_send, t_recv
+    )
+    for g in range(2):
+        tbuf[3, g, HALO + w] = tsend[3, g, w]
+    receive(2, there_up)
     loads[6].wait()
     for copy in ag_h:
         copy.wait_recv()
@@ -216,52 +263,24 @@
     for j in range(3):
         tsend[j] = dot(h_all, wt[j]).astype(BF16).reshape(2, PL, 16, LW)
 
-    there = []
-    for g in range(2):
-        for k in range(1, PL):
-            to = lax.rem(w + k, PL)
-            copy = remote(
-                tsend.at[:, g, to], tbuf.at[:, g, HALO + w],
-                t_send.at[g, k - 1], t_recv.at[g, k - 1], zpos * PL + to, m,
-            )
-            copy.start()
-            there.append(copy)
-    pending.extend(there)
-    for t in range(4):
+    there = [
+        plane_send(g, lambda to, g=g: tsend.at[:3, g, to], halo_view(g, HALO + w), t_send, t_recv)
+        for g in range(2)
+    ]
+    for t in range(3):
         for g in range(2):
             tbuf[t, g, HALO + w] = tsend[t, g, w]
 
-    def hand_on(g, frame):
-        def to_plane(step, slot):
-            return remote(
-                tbuf.at[:, g, HALO + frame], tbuf.at[:, g, slot],
-                h_send.at[g], h_recv.at[g], lax.rem(zpos + step, ZS) * PL + w, m,
-            )
-
-        @pl.when(frame < HALO)
-        def _():
-            to_plane(ZS - 1, HALO + PL + frame).start()
-
-        @pl.when(frame >= PL - HALO)
-        def _():
-            to_plane(1, frame - (PL - HALO)).start()
-
-    def hand_wait(g):
-        some = pl.ds(0, 2 * HALO)
-        return remote(
-            tbuf.at[:, g, some], tbuf.at[:, g, some], h_send.at[g], h_recv.at[g], f, m
-        )
-
     for g in range(2):
-        hand_on(g, w)
-        for k in range(1, PL):
-            there[g * (PL - 1) + k - 1].wait_recv()
-            hand_on(g, lax.rem(w + PL - k, PL))
+        receive(g, there[g])
 
     zero = jnp.zeros((LW, LW), F32)
+    own_slots = slice(HALO, HALO + PL)
     back = []
     for g in range(2):
         hand_wait(g).wait_recv()
+        if g == 0:
+            hand_wait(2).wait_recv()
         queries, keys, values, upstream = [tbuf[t, g].reshape(LW, LW) for t in range(4)]
         attn_t, d_q, d_k, d_v = zero, zero, zero, zero
         for h in range(HEADS_LOC):
@@ -275,19 +294,13 @@
             d_q = d_q + dot(ds, keys * masks[h])
             d_k = d_k + dot_at(ds, qm)
         for t, full in enumerate((d_q, d_k, d_v, attn_t)):
-            mine = full[16 * HALO : 16 * (HALO + PL)]
-            tres[t, g] = mine.astype(BF16).reshape(PL, 16, LW)
-        for k in range(1, PL):
-            to = lax.rem(w + k, PL)
-            copy = remote(
-                tres.at[:, g, to], dqkv.at[:, g, w],
-                b_send.at[g, k - 1], b_recv.at[g, k - 1], zpos * PL + to, m,
-            )
-            copy.start()
-            back.append(copy)
+            tres[t, g] = full.astype(BF16).reshape(16, 16, LW)[own_slots]
+        back += plane_send(
+            g, lambda to, g=g: tres.at[:3, g, to], dqkv.at[:3, g, w], b_send, b_recv
+        )
         for t in range(4):
             dqkv[t, g, w] = tres[t, g, w]
-    pending.extend(back)
+    back_attn = plane_send(2, lambda to: tres.at[3, :, to], dqkv.at[3, :, w], b_send, b_recv)
     for copy in back:
         copy.wait_recv()
 
@@ -373,15 +386,18 @@
                 summed = summed + grecv3[k, j].astype(F32)
             out[...] = summed
 
-    grads_t = [dqkv[j].reshape(LW, LW) for j in range(4)]
-    project_back(1, grads_t[:3], wt)
+    grads_t = [dqkv[j].reshape(LW, LW) for j in range(3)]
+    project_back(1, grads_t, wt)
     rs2 = scatter_mp(4, 1)
     for j in range(3):
         weight_grad(j, nhall, grads_t[j])
-    weight_grad(3, gall, grads_t[3])
+    for copy in back_attn:
+        copy.wait_recv()
+    weight_grad(3, gall, dqkv[3].reshape(LW, LW))
     core_t = core_send(0)
     half = pl.ds(4 * lax.rem(m, 2), 4)
     d_nh = own_back([dqkv[j, m // 2, half].reshape(ROWS, LW) for j in range(3)], wt)
+    x_t = core_sum_x_send(0, core_t)
     for copy in rs2:
         copy.wait_recv()
     for k in range(3):
@@ -392,7 +408,6 @@
     dhid[...] = d_hidden
     dhall[m] = d_hidden.astype(BF16)
     ag_d = gather_mp(5, dhall.at[m], dhall)
-    x_t = core_sum_x_send(0, core_t)
     for copy in ag_d:
         copy.wait_recv()
 
@@ -442,8 +457,8 @@
     z_sum(2, z_k, [gs_ref.at[1]])
     for copy in pending:
         copy.wait_send()
-    for g in range(2):
-        hand_wait(g).wait_send()
+    for part in range(3):
+        hand_wait(part).wait_send()
 
 
 def deliver(*refs):
@@ -487,14 +502,14 @@
         pltpu.VMEM((8, ZS, 16, LW), BF16),
         pltpu.VMEM((ZS - 1, 8, 16, LW), BF16),
         dma((7,)),
-        dma((7, 3)),
-        dma((7, 3)),
-        dma((2, PL - 1)),
-        dma((2, PL - 1)),
-        dma((2,)),
-        dma((2,)),
-        dma((2, PL - 1)),
-        dma((2, PL - 1)),
+        dma((8, 3)),
+        dma((8, 3)),
+        dma((3, PL - 1)),
+        dma((3, PL - 1)),
+        dma((3,)),
+        dma((3,)),
+        dma((3, PL - 1)),
+        dma((3, PL - 1)),
         dma((5,)),
         dma((5,)),
         dma((5, XS - 1)),

time: 101 us -> 98 us (0.970); the launches traced: 99 us -> 97.1 us
  Pallas kernels: 98.4 us -> 96.5 us
    pallas_call x1, Pallas kernels: 96.7 us -> 94.8 us  [shards(): pl.pallas_call(kernel, out_shape=(jax.ShapeDtypeStruct((ROWS, D), BF16),...]
where the time goes in v4:
time: 98 us; the launch traced here: 97.1 us
  Pallas kernels  96.5 us (98%)
    pallas_call x1, Pallas kernels, shards(): pl.pallas_call(kernel, out_shape=(jax.ShapeDtypeStruct((ROWS, D), BF16),...  94.8 us

profile of v4, /device:TPU:8, one launch (start us, length us, event | category | flops | bytes accessed | tf_op | source)
XLA Modules:
  0.0 97.1 jit_solution(7403740027359069713)
XLA Ops:
  0.6 94.8 %shard_map.110 = (bf16[64,1024]{1,0:T(8,128)(2,1)}, f32[3,16,256]{2,1,0:T(8,128)}, f32[16,256]{1,0:T(8,128)}, f32[3,16,256]{2,1,0:T(8,128)}, f32[16,256]{1,0:T(8,128)}) custom-call(bf16[64,1024]{1,0:T(8,128)(2,1)} %bitcast.6, bf16[64,1024]{1,0:T(8,128)(2,1)} %bitcast.7, s32[1,32]{1,0:T(1,128)} %bitcast.11, bf16[3,1024,256]{2,1,0:T(8,128)(2,1)} %ws_hbm.1, ...), custom_call_target="tpu_custom_call" | custom-call | flops 3500000000 | bytes 6000000 | tf_op jit(solution)/shard_map/pallas_call | solution.py:520
  95.5 1.7 %shard_map.111 = (bf16[64,1024]{1,0:T(8,128)(2,1)}, f32[3,16,256]{2,1,0:T(8,128)}, f32[16,256]{1,0:T(8,128)}, f32[3,16,256]{2,1,0:T(8,128)}, f32[16,256]{1,0:T(8,128)}) custom-call(bf16[64,1024]{1,0:T(8,128)(2,1)} %get-tuple-element.15.refs_0_, f32[3,16,256]{2,1,0:T(8,128)} %get-tuple-element.16.refs_1_, f32[16,256]{1,0:T(8,128)} %get-tuple-element.17.refs_2_, ...), custom_call_target="tpu_custom_call" | custom-call | tf_op jit(solution)/shard_map/pallas_call | solution.py:542

commit v5 on v4

--- a/solution.py
+++ b/solution.py
@@ -61,7 +61,7 @@
     x_ref, g_ref, cf_row, ws, wos, wt, wot, xall, gall, nhall, dhall,
     bias, qkvs, probs, attns, hid, dhid,
     rsend, rrecv, tsend, tbuf, tres, dqkv, dqs,
-    gbuf, grecv1, gsum1, grecv2, gsum2, grecv3,
+    gbuf, grecv1, gsum1, grecv2, gsum2, grecv3, hrecv2, hsum2, hrecv3,
     w_sem, mp_send, mp_recv, t_send, t_recv, h_send, h_recv, b_send, b_recv,
     c_send, c_recv, x_send, x_recv, z_send, z_recv,
 ):
@@ -119,12 +119,12 @@
         pending.extend(copies)
         return copies
 
-    def scatter_mp(phase, which):
+    def scatter_mp(phase, which, rows=slice(0, ROWS)):
         copies = []
         for k in (1, 3, 2):
             to = lax.rem(m + k, MP)
             copy = remote(
-                rsend.at[which, to], rrecv.at[which, k - 1],
+                rsend.at[which, to, rows], rrecv.at[which, k - 1, rows],
                 mp_send.at[phase, k - 1], mp_recv.at[phase, k - 1], f, to,
             )
             copy.start()
@@ -169,6 +169,7 @@
         for g in range(2):
             tbuf[t, g, used:] = jnp.zeros((16 - used, 16, LW), BF16)
 
+    halves = [slice(0, ROWS // 2), slice(ROWS // 2, ROWS)]
     masks = [head_mask(h) for h in range(HEADS_LOC)]
 
     loads[3].wait()
@@ -191,19 +192,21 @@
     for c in range(4):
         cols = pl.ds(c * 256, 256)
         rsend[0, :, :, cols] = dot(attn, wos[:, cols]).astype(BF16).reshape(MP, ROWS, 256)
-    rs1 = scatter_mp(2, 0)
+    rs1 = [scatter_mp(p, 0, rows) for p, rows in zip((2, 8), halves)]
     ag_g = ag_g + gather_mp(7, g_ref, gall, slice(ROWS // 2, ROWS))
     own = dot(attns[m], wos[...])
 
-    for copy in rs1:
-        copy.wait_recv()
-    hidden = x_ref[...].astype(F32) + own
-    for k in range(3):
-        hidden = hidden + rrecv[0, k].astype(F32)
-    inv_h = lax.rsqrt(jnp.mean(hidden * hidden, -1, keepdims=True) + EPS)
-    hid[...] = hidden
-    nhall[m] = (hidden * inv_h).astype(BF16)
-    ag_h = gather_mp(3, nhall.at[m], nhall)
+    ag_h = []
+    for at, rows in enumerate(halves):
+        for copy in rs1[at]:
+            copy.wait_recv()
+        hidden = x_ref[rows].astype(F32) + own[rows]
+        for k in range(3):
+            hidden = hidden + rrecv[0, k, rows].astype(F32)
+        inv_h = lax.rsqrt(jnp.mean(hidden * hidden, -1, keepdims=True) + EPS)
+        hid[rows] = hidden
+        nhall[m, rows] = (hidden * inv_h).astype(BF16)
+        ag_h += gather_mp((3, 9)[at], nhall.at[m], nhall, rows)
 
     def plane_send(part, source, target, ssems, rsems):
         copies = []
@@ -322,8 +325,8 @@
             left = left_ref[:, :, c * 256 : (c + 1) * 256].reshape(LW, 256)
             gbuf[j, 8 * c : 8 * c + 8] = dot_at(left, right).astype(BF16).reshape(8, 2, 16, LW)
 
-    first = [0, 4, 5, 6, 7]
-    count = [4, 1, 1, 1, 1]
+    first = [0, 2, 4, 5, 6, 7]
+    count = [2, 2, 1, 1, 1, 1]
 
     def core_send(b):
         some = slice(first[b], first[b] + count[b])
@@ -335,18 +338,12 @@
         pending.append(copy)
         return copy
 
-    def core_sum_x_send(b, copy):
-        copy.wait_recv()
-        some = slice(first[b], first[b] + count[b])
-        for j in range(some.start, some.stop):
-            summed = gbuf[j, :, core].astype(F32) + grecv1[j].astype(F32)
-            gsum1[j] = summed.astype(BF16).reshape(ZS, XS, 16, LW)
+    def send_x(b, source, target):
         copies = []
         for k in (1, 3, 2):
             to = lax.rem(xpos + k, XS)
             copy = remote(
-                gsum1.at[some, :, to], grecv2.at[k - 1, some],
-                x_send.at[b, k - 1], x_recv.at[b, k - 1],
+                source(to), target(k - 1), x_send.at[b, k - 1], x_recv.at[b, k - 1],
                 (zpos * XS + to) * 2 + core, m,
             )
             copy.start()
@@ -354,21 +351,12 @@
         pending.extend(copies)
         return copies
 
-    def x_sum_z_send(b, copies):
-        for copy in copies:
-            copy.wait_recv()
-        some = slice(first[b], first[b] + count[b])
-        for j in range(some.start, some.stop):
-            summed = gsum1[j, :, xpos].astype(F32)
-            for k in range(3):
-                summed = summed + grecv2[k, j].astype(F32)
-            gsum2[j] = summed.astype(BF16)
+    def send_z(b, source, target):
         copies = []
         for k in (4, 3, 5, 2, 6, 1, 7):
             to = lax.rem(zpos + k, ZS)
             copy = remote(
-                gsum2.at[some, to], grecv3.at[k - 1, some],
-                z_send.at[b, k - 1], z_recv.at[b, k - 1],
+                source(to), target(k - 1), z_send.at[b, k - 1], z_recv.at[b, k - 1],
                 (to * XS + xpos) * 2 + core, m,
             )
             copy.start()
@@ -376,9 +364,47 @@
         pending.extend(copies)
         return copies
 
-    def z_sum(b, copies, outs):
+    def mats(b):
+        return slice(first[b], first[b] + count[b])
+
+    def wait_all(copies):
         for copy in copies:
             copy.wait_recv()
+
+    def core_sum(b, copy):
+        copy.wait_recv()
+        for j in range(first[b], first[b] + count[b]):
+            summed = gbuf[j, :, core].astype(F32) + grecv1[j].astype(F32)
+            gsum1[j] = summed.astype(BF16).reshape(ZS, XS, 16, LW)
+
+    def core_sum_x_send(b, copy):
+        core_sum(b, copy)
+        return send_x(b, lambda to: gsum1.at[mats(b), :, to], lambda k: grecv2.at[k, mats(b)])
+
+    def core_sum_z_send(b, copy):
+        core_sum(b, copy)
+        return send_z(b, lambda to: gsum1.at[mats(b), to], lambda k: hrecv2.at[k, mats(b)])
+
+    def x_sum_z_send(b, copies):
+        wait_all(copies)
+        for j in range(first[b], first[b] + count[b]):
+            summed = gsum1[j, :, xpos].astype(F32)
+            for k in range(XS - 1):
+                summed = summed + grecv2[k, j].astype(F32)
+            gsum2[j] = summed.astype(BF16)
+        return send_z(b, lambda to: gsum2.at[mats(b), to], lambda k: grecv3.at[k, mats(b)])
+
+    def z_sum_x_send(b, copies):
+        wait_all(copies)
+        for j in range(first[b], first[b] + count[b]):
+            summed = gsum1[j, zpos].astype(F32)
+            for k in range(ZS - 1):
+                summed = summed + hrecv2[k, j].astype(F32)
+            hsum2[j] = summed.astype(BF16)
+        return send_x(b, lambda to: hsum2.at[mats(b), to], lambda k: hrecv3.at[k, mats(b)])
+
+    def z_sum(b, copies, outs):
+        wait_all(copies)
         for at, out in enumerate(outs):
             j = first[b] + at
             summed = gsum2[j, zpos].astype(F32)
@@ -386,45 +412,58 @@
                 summed = summed + grecv3[k, j].astype(F32)
             out[...] = summed
 
+    def x_sum(b, copies, outs):
+        wait_all(copies)
+        for at, out in enumerate(outs):
+            j = first[b] + at
+            summed = hsum2[j, xpos].astype(F32)
+            for k in range(XS - 1):
+                summed = summed + hrecv3[k, j].astype(F32)
+            out[...] = summed
+
     grads_t = [dqkv[j].reshape(LW, LW) for j in range(3)]
     project_back(1, grads_t, wt)
-    rs2 = scatter_mp(4, 1)
-    for j in range(3):
+    rs2 = [scatter_mp(p, 1, rows) for p, rows in zip((4, 10), halves)]
+    for j in range(2):
         weight_grad(j, nhall, grads_t[j])
-    for copy in back_attn:
-        copy.wait_recv()
+    core_t1 = core_send(0)
+    weight_grad(2, nhall, grads_t[2])
+    wait_all(back_attn)
     weight_grad(3, gall, dqkv[3].reshape(LW, LW))
-    core_t = core_send(0)
-    half = pl.ds(4 * lax.rem(m, 2), 4)
-    d_nh = own_back([dqkv[j, m // 2, half].reshape(ROWS, LW) for j in range(3)], wt)
-    x_t = core_sum_x_send(0, core_t)
-    for copy in rs2:
-        copy.wait_recv()
-    for k in range(3):
-        d_nh = d_nh + rrecv[1, k].astype(F32)
-    hidden = hid[...]
-    inv_h = lax.rsqrt(jnp.mean(hidden * hidden, -1, keepdims=True) + EPS)
-    d_hidden = g_ref[...].astype(F32) + norm_back(hidden, inv_h, d_nh)
-    dhid[...] = d_hidden
-    dhall[m] = d_hidden.astype(BF16)
-    ag_d = gather_mp(5, dhall.at[m], dhall)
-    for copy in ag_d:
-        copy.wait_recv()
+    core_t2 = core_send(1)
+    quarter = pl.ds(4 * lax.rem(m, 2), 4)
+    own = own_back([dqkv[j, m // 2, quarter].reshape(ROWS, LW) for j in range(3)], wt)
+    x_t1 = core_sum_x_send(0, core_t1)
+    z_t2 = core_sum_z_send(1, core_t2)
+    ag_d = []
+    for at, rows in enumerate(halves):
+        wait_all(rs2[at])
+        d_nh = own[rows]
+        for k in range(3):
+            d_nh = d_nh + rrecv[1, k, rows].astype(F32)
+        hidden = hid[rows]
+        inv_h = lax.rsqrt(jnp.mean(hidden * hidden, -1, keepdims=True) + EPS)
+        d_hidden = g_ref[rows].astype(F32) + norm_back(hidden, inv_h, d_nh)
+        dhid[rows] = d_hidden
+        dhall[m, rows] = d_hidden.astype(BF16)
+        ag_d += gather_mp((5, 11)[at], dhall.at[m], dhall, rows)
+    z_t1 = x_sum_z_send(0, x_t1)
+    wait_all(ag_d)
 
     weight_grad(7, dhall, attns[...].reshape(LW, LW))
-    core_o = core_send(4)
+    core_o = core_send(5)
     das = dot_bt(dhall[...].reshape(LW, D), wos[...]).astype(BF16)
 
     def keep(j, grad):
         dqs[j] = grad.astype(BF16).reshape(MP, ROWS, LW)
         weight_grad(4 + j, xall, dqs[j].reshape(LW, LW))
-        return core_send(1 + j)
+        return core_send(2 + j)
 
     d_v = zero
     for h in range(HEADS_LOC):
         d_v = d_v + dot_at(probs[h].astype(BF16), das * masks[h])
     core_v = keep(2, d_v)
-    x_o = core_sum_x_send(4, core_o)
+    x_o = core_sum_x_send(5, core_o)
     d_q, d_k = zero, zero
     for h in range(HEADS_LOC):
         ds = score_grads(probs[h], dot_bt(das * masks[h], qkvs[2]))
@@ -432,29 +471,29 @@
         d_k = d_k + dot_at(ds, qkvs[0] * masks[h])
     core_q = keep(0, d_q)
     core_k = keep(1, d_k)
-    x_v = core_sum_x_send(3, core_v)
-    z_t = x_sum_z_send(0, x_t)
-    x_q = core_sum_x_send(1, core_q)
-    x_k = core_sum_x_send(2, core_k)
+    z_v = core_sum_z_send(4, core_v)
+    x_q = core_sum_x_send(2, core_q)
+    x_k = core_sum_x_send(3, core_k)
     project_back(2, [dqs[j].reshape(LW, LW) for j in range(3)], ws)
     rs3 = scatter_mp(6, 2)
-    z_o = x_sum_z_send(4, x_o)
-    z_v = x_sum_z_send(3, x_v)
-    z_sum(0, z_t, [gt_ref.at[0], gt_ref.at[1], gt_ref.at[2], gto_ref])
+    x_t2 = z_sum_x_send(1, z_t2)
+    z_o = x_sum_z_send(5, x_o)
+    z_sum(0, z_t1, [gt_ref.at[0], gt_ref.at[1]])
     d_nx = own_back([dqs[j, m] for j in range(3)], ws)
-    z_q = x_sum_z_send(1, x_q)
-    for copy in rs3:
-        copy.wait_recv()
+    z_q = x_sum_z_send(2, x_q)
+    x_sum(1, x_t2, [gt_ref.at[2], gto_ref])
+    z_k = x_sum_z_send(3, x_k)
+    x_v = z_sum_x_send(4, z_v)
+    wait_all(rs3)
     for k in range(3):
         d_nx = d_nx + rrecv[2, k].astype(F32)
     x = x_ref[...].astype(F32)
     inv_x = lax.rsqrt(jnp.mean(x * x, -1, keepdims=True) + EPS)
     tok_ref[...] = (dhid[...] + norm_back(x, inv_x, d_nx)).astype(BF16)
-    z_k = x_sum_z_send(2, x_k)
-    z_sum(4, z_o, [gso_ref])
-    z_sum(3, z_v, [gs_ref.at[2]])
-    z_sum(1, z_q, [gs_ref.at[0]])
-    z_sum(2, z_k, [gs_ref.at[1]])
+    z_sum(5, z_o, [gso_ref])
+    x_sum(4, x_v, [gs_ref.at[2]])
+    z_sum(2, z_q, [gs_ref.at[0]])
+    z_sum(3, z_k, [gs_ref.at[1]])
     for copy in pending:
         copy.wait_send()
     for part in range(3):
@@ -501,21 +540,24 @@
         pltpu.VMEM((XS - 1, 8, ZS, 16, LW), BF16),
         pltpu.VMEM((8, ZS, 16, LW), BF16),
         pltpu.VMEM((ZS - 1, 8, 16, LW), BF16),
+        pltpu.VMEM((ZS - 1, 8, XS, 16, LW), BF16),
+        pltpu.VMEM((8, XS, 16, LW), BF16),
+        pltpu.VMEM((XS - 1, 8, 16, LW), BF16),
         dma((7,)),
-        dma((8, 3)),
-        dma((8, 3)),
+        dma((12, 3)),
+        dma((12, 3)),
         dma((3, PL - 1)),
         dma((3, PL - 1)),
         dma((3,)),
         dma((3,)),
         dma((3, PL - 1)),
         dma((3, PL - 1)),
-        dma((5,)),
-        dma((5,)),
-        dma((5, XS - 1)),
-        dma((5, XS - 1)),
-        dma((5, ZS - 1)),
-        dma((5, ZS - 1)),
+        dma((6,)),
+        dma((6,)),
+        dma((6, XS - 1)),
+        dma((6, XS - 1)),
+        dma((6, ZS - 1)),
+        dma((6, ZS - 1)),
     ]
     tokens, gs, gso, gt, gto = pl.pallas_call(
         kernel,

time: 98 us -> 94.9 us (0.968)
  Pallas kernels: 96.5 us -> 93.3 us
    pallas_call x1, Pallas kernels: 94.8 us -> 91.6 us  [shards(): pl.pallas_call(kernel, out_shape=(jax.ShapeDtypeStruct((ROWS, D), BF16),...]
where the time goes in v5:
time: 94.9 us; the launch traced here: 93.9 us
  Pallas kernels  93.3 us (98%)
    pallas_call x1, Pallas kernels, shards(): pl.pallas_call(kernel, out_shape=(jax.ShapeDtypeStruct((ROWS, D), BF16),...  91.6 us

profile of v5, /device:TPU:8, one launch (start us, length us, event | category | flops | bytes accessed | tf_op | source)
XLA Modules:
  0.0 93.9 jit_solution(13583468631018007841)
XLA Ops:
  0.6 91.6 %shard_map.110 = (bf16[64,1024]{1,0:T(8,128)(2,1)}, f32[3,16,256]{2,1,0:T(8,128)}, f32[16,256]{1,0:T(8,128)}, f32[3,16,256]{2,1,0:T(8,128)}, f32[16,256]{1,0:T(8,128)}) custom-call(bf16[64,1024]{1,0:T(8,128)(2,1)} %bitcast.6, bf16[64,1024]{1,0:T(8,128)(2,1)} %bitcast.7, s32[1,32]{1,0:T(1,128)} %bitcast.11, bf16[3,1024,256]{2,1,0:T(8,128)(2,1)} %ws_hbm.1, ...), custom_call_target="tpu_custom_call" | custom-call | flops 3500000000 | bytes 6000000 | tf_op jit(solution)/shard_map/pallas_call | solution.py:562
  92.3 1.7 %shard_map.111 = (bf16[64,1024]{1,0:T(8,128)(2,1)}, f32[3,16,256]{2,1,0:T(8,128)}, f32[16,256]{1,0:T(8,128)}, f32[3,16,256]{2,1,0:T(8,128)}, f32[16,256]{1,0:T(8,128)}) custom-call(bf16[64,1024]{1,0:T(8,128)(2,1)} %get-tuple-element.15.refs_0_, f32[3,16,256]{2,1,0:T(8,128)} %get-tuple-element.16.refs_1_, f32[16,256]{1,0:T(8,128)} %get-tuple-element.17.refs_2_, ...), custom_call_target="tpu_custom_call" | custom-call | tf_op jit(solution)/shard_map/pallas_call | solution.py:584

commit v6 on v5

--- a/solution.py
+++ b/solution.py
@@ -175,7 +175,13 @@
     loads[3].wait()
     for copy in ag_x:
         copy.wait_recv()
-    ag_g = gather_mp(1, g_ref, gall, slice(0, ROWS // 2))
+    near_g = {}
+    for k in (1, 3):
+        near_g[k] = remote(
+            g_ref, gall.at[m], mp_send.at[1, k - 1], mp_recv.at[1, k - 1], f, lax.rem(m + k, MP)
+        )
+        near_g[k].start()
+        pending.append(near_g[k])
     x_all = xall[...].reshape(LW, D)
     for j in range(3):
         qkvs[j] = dot(x_all, ws[j]).astype(BF16)
@@ -193,8 +199,17 @@
         cols = pl.ds(c * 256, 256)
         rsend[0, :, :, cols] = dot(attn, wos[:, cols]).astype(BF16).reshape(MP, ROWS, 256)
     rs1 = [scatter_mp(p, 0, rows) for p, rows in zip((2, 8), halves)]
-    ag_g = ag_g + gather_mp(7, g_ref, gall, slice(ROWS // 2, ROWS))
     own = dot(attns[m], wos[...])
+    far_g = []
+    for k, rows in zip((1, 3), halves):
+        near_g[k].wait_recv()
+        chunk = gall.at[lax.rem(m + MP - k, MP), rows]
+        copy = remote(
+            chunk, chunk, mp_send.at[7, k - 1], mp_recv.at[7, k - 1], f, lax.rem(m + k, MP)
+        )
+        copy.start()
+        far_g.append(copy)
+    pending.extend(far_g)
 
     ag_h = []
     for at, rows in enumerate(halves):
@@ -250,7 +265,7 @@
             hand_on(part, lax.rem(w + PL - k, PL))
 
     loads[5].wait()
-    for copy in ag_g:
+    for copy in far_g:
         copy.wait_recv()
     tsend[3] = dot_bt(gall[...].reshape(LW, D), wot[...]).astype(BF16).reshape(2, PL, 16, LW)
     there_up = plane_send(

time: 94.9 us -> 93.6 us (0.986)
  Pallas kernels: 93.3 us -> 92 us
    pallas_call x1, Pallas kernels: 91.6 us -> 90.3 us  [shards(): pl.pallas_call(kernel, out_shape=(jax.ShapeDtypeStruct((ROWS, D), BF16),...]
where the time goes in v6:
time: 93.6 us; the launch traced here: 92.6 us
  Pallas kernels  92 us (98%)
    pallas_call x1, Pallas kernels, shards(): pl.pallas_call(kernel, out_shape=(jax.ShapeDtypeStruct((ROWS, D), BF16),...  90.3 us

profile of v6, /device:TPU:8, one launch (start us, length us, event | category | flops | bytes accessed | tf_op | source)
XLA Modules:
  0.0 92.6 jit_solution(5975611372909458529)
XLA Ops:
  0.6 90.3 %shard_map.110 = (bf16[64,1024]{1,0:T(8,128)(2,1)}, f32[3,16,256]{2,1,0:T(8,128)}, f32[16,256]{1,0:T(8,128)}, f32[3,16,256]{2,1,0:T(8,128)}, f32[16,256]{1,0:T(8,128)}) custom-call(bf16[64,1024]{1,0:T(8,128)(2,1)} %bitcast.6, bf16[64,1024]{1,0:T(8,128)(2,1)} %bitcast.7, s32[1,32]{1,0:T(1,128)} %bitcast.11, bf16[3,1024,256]{2,1,0:T(8,128)(2,1)} %ws_hbm.1, ...), custom_call_target="tpu_custom_call" | custom-call | flops 3500000000 | bytes 6000000 | tf_op jit(solution)/shard_map/pallas_call | solution.py:577
  91.0 1.7 %shard_map.111 = (bf16[64,1024]{1,0:T(8,128)(2,1)}, f32[3,16,256]{2,1,0:T(8,128)}, f32[16,256]{1,0:T(8,128)}, f32[3,16,256]{2,1,0:T(8,128)}, f32[16,256]{1,0:T(8,128)}) custom-call(bf16[64,1024]{1,0:T(8,128)(2,1)} %get-tuple-element.15.refs_0_, f32[3,16,256]{2,1,0:T(8,128)} %get-tuple-element.16.refs_1_, f32[16,256]{1,0:T(8,128)} %get-tuple-element.17.refs_2_, ...), custom_call_target="tpu_custom_call" | custom-call | tf_op jit(solution)/shard_map/pallas_call | solution.py:599

commit v7 on v6

--- a/solution.py
+++ b/solution.py
@@ -59,7 +59,7 @@
     x_hbm, g_hbm, cf_hbm, ws_hbm, wos_hbm, wt_hbm, wot_hbm,
     tok_ref, gs_ref, gso_ref, gt_ref, gto_ref,
     x_ref, g_ref, cf_row, ws, wos, wt, wot, xall, gall, nhall, dhall,
-    bias, qkvs, probs, attns, hid, dhid,
+    bias, qkvs, probs, x_turned, p_turned, attns, hid, dhid,
     rsend, rrecv, tsend, tbuf, tres, dqkv, dqs,
     gbuf, grecv1, gsum1, grecv2, gsum2, grecv3, hrecv2, hsum2, hrecv3,
     w_sem, mp_send, mp_recv, t_send, t_recv, h_send, h_recv, b_send, b_recv,
@@ -200,6 +200,10 @@
         rsend[0, :, :, cols] = dot(attn, wos[:, cols]).astype(BF16).reshape(MP, ROWS, 256)
     rs1 = [scatter_mp(p, 0, rows) for p, rows in zip((2, 8), halves)]
     own = dot(attns[m], wos[...])
+    for c in range(4):
+        x_turned[c] = xall[:, :, c * 256 : (c + 1) * 256].reshape(LW, 256).T
+    for h in range(HEADS_LOC):
+        p_turned[h] = probs[h].astype(BF16).T
     far_g = []
     for k, rows in zip((1, 3), halves):
         near_g[k].wait_recv()
@@ -339,6 +343,11 @@
         for c in range(4):
             left = left_ref[:, :, c * 256 : (c + 1) * 256].reshape(LW, 256)
             gbuf[j, 8 * c : 8 * c + 8] = dot_at(left, right).astype(BF16).reshape(8, 2, 16, LW)
+
+    def weight_grad_x(j, right):
+        for c in range(4):
+            part = dot(x_turned[c], right)
+            gbuf[j, 8 * c : 8 * c + 8] = part.astype(BF16).reshape(8, 2, 16, LW)
 
     first = [0, 2, 4, 5, 6, 7]
     count = [2, 2, 1, 1, 1, 1]
@@ -471,12 +480,12 @@
 
     def keep(j, grad):
         dqs[j] = grad.astype(BF16).reshape(MP, ROWS, LW)
-        weight_grad(4 + j, xall, dqs[j].reshape(LW, LW))
+        weight_grad_x(4 + j, dqs[j].reshape(LW, LW))
         return core_send(2 + j)
 
     d_v = zero
     for h in range(HEADS_LOC):
-        d_v = d_v + dot_at(probs[h].astype(BF16), das * masks[h])
+        d_v = d_v + dot(p_turned[h], das * masks[h])
     core_v = keep(2, d_v)
     x_o = core_sum_x_send(5, core_o)
     d_q, d_k = zero, zero
@@ -484,9 +493,9 @@
         ds = score_grads(probs[h], dot_bt(das * masks[h], qkvs[2]))
         d_q = d_q + dot(ds, qkvs[1] * masks[h])
         d_k = d_k + dot_at(ds, qkvs[0] * masks[h])
+    z_v = core_sum_z_send(4, core_v)
     core_q = keep(0, d_q)
     core_k = keep(1, d_k)
-    z_v = core_sum_z_send(4, core_v)
     x_q = core_sum_x_send(2, core_q)
     x_k = core_sum_x_send(3, core_k)
     project_back(2, [dqs[j].reshape(LW, LW) for j in range(3)], ws)
@@ -539,6 +548,8 @@
         pltpu.VMEM((LW, LW), F32),
         pltpu.VMEM((3, LW, LW), BF16),
         pltpu.VMEM((HEADS_LOC, LW, LW), F32),
+        pltpu.VMEM((4, LW, LW), BF16),
+        pltpu.VMEM((HEADS_LOC, LW, LW), BF16),
         pltpu.VMEM((MP, ROWS, LW), BF16),
         pltpu.VMEM((ROWS, D), F32),
         pltpu.VMEM((ROWS, D), F32),

time: 93.6 us -> 93.8 us (level)
  no operation moved by 1% of the time
where the time goes in v7:
time: 93.8 us; the launch traced here: 92.8 us
  Pallas kernels  92.2 us (98%)
    pallas_call x1, Pallas kernels, shards(): pl.pallas_call(kernel, out_shape=(jax.ShapeDtypeStruct((ROWS, D), BF16),...  90.5 us

profile of v7, /device:TPU:8, one launch (start us, length us, event | category | flops | bytes accessed | tf_op | source)
XLA Modules:
  0.0 92.8 jit_solution(15174273226031703627)
XLA Ops:
  0.6 90.5 %shard_map.110 = (bf16[64,1024]{1,0:T(8,128)(2,1)}, f32[3,16,256]{2,1,0:T(8,128)}, f32[16,256]{1,0:T(8,128)}, f32[3,16,256]{2,1,0:T(8,128)}, f32[16,256]{1,0:T(8,128)}) custom-call(bf16[64,1024]{1,0:T(8,128)(2,1)} %bitcast.6, bf16[64,1024]{1,0:T(8,128)(2,1)} %bitcast.7, s32[1,32]{1,0:T(1,128)} %bitcast.11, bf16[3,1024,256]{2,1,0:T(8,128)(2,1)} %ws_hbm.1, ...), custom_call_target="tpu_custom_call" | custom-call | flops 3500000000 | bytes 6000000 | tf_op jit(solution)/shard_map/pallas_call | solution.py:588
  91.2 1.7 %shard_map.111 = (bf16[64,1024]{1,0:T(8,128)(2,1)}, f32[3,16,256]{2,1,0:T(8,128)}, f32[16,256]{1,0:T(8,128)}, f32[3,16,256]{2,1,0:T(8,128)}, f32[16,256]{1,0:T(8,128)}) custom-call(bf16[64,1024]{1,0:T(8,128)(2,1)} %get-tuple-element.15.refs_0_, f32[3,16,256]{2,1,0:T(8,128)} %get-tuple-element.16.refs_1_, f32[16,256]{1,0:T(8,128)} %get-tuple-element.17.refs_2_, ...), custom_call_target="tpu_custom_call" | custom-call | tf_op jit(solution)/shard_map/pallas_call | solution.py:610

commit v8 on v7

--- a/solution.py
+++ b/solution.py
@@ -57,7 +57,8 @@
 
 def kernel(
     x_hbm, g_hbm, cf_hbm, ws_hbm, wos_hbm, wt_hbm, wot_hbm,
-    tok_ref, gs_ref, gso_ref, gt_ref, gto_ref,
+    tok_out, gs_out, gso_out, gt_out, gto_out,
+    tok_ref, gs_ref, gso_ref, gt_ref, gto_ref, out_sem,
     x_ref, g_ref, cf_row, ws, wos, wt, wot, xall, gall, nhall, dhall,
     bias, qkvs, probs, x_turned, p_turned, attns, hid, dhid,
     rsend, rrecv, tsend, tbuf, tres, dqkv, dqs,
@@ -323,8 +324,6 @@
         for t in range(4):
             dqkv[t, g, w] = tres[t, g, w]
     back_attn = plane_send(2, lambda to: tres.at[3, :, to], dqkv.at[3, :, w], b_send, b_recv)
-    for copy in back:
-        copy.wait_recv()
 
     def project_back(which, grads, weights):
         for c in range(4):
@@ -445,9 +444,34 @@
                 summed = summed + hrecv3[k, j].astype(F32)
             out[...] = summed
 
+    rs2 = []
+    for phase, rows in zip((4, 10), halves):
+        copies = []
+        for k in (1, 3, 2):
+            to = lax.rem(m + k, MP)
+            copies.append(remote(
+                rsend.at[1, to, rows], rrecv.at[1, k - 1, rows],
+                mp_send.at[phase, k - 1], mp_recv.at[phase, k - 1], f, to,
+            ))
+        rs2.append(copies)
+        pending.extend(copies)
+    for g in range(2):
+        wait_all(back[g * (PL - 1) : (g + 1) * (PL - 1)])
+        grads = [dqkv[j, g].reshape(LW // 2, LW) for j in range(3)]
+        for c in range(4):
+            cols = pl.ds(c * 256, 256)
+            part = dot_bt(grads[0], wt[0, cols])
+            part = part + dot_bt(grads[1], wt[1, cols])
+            part = part + dot_bt(grads[2], wt[2, cols])
+            rsend[1, 2 * g : 2 * g + 2, :, cols] = part.astype(BF16).reshape(2, ROWS, 256)
+        for copies in rs2:
+            for k, copy in zip((1, 3, 2), copies):
+
+                @pl.when(lax.rem(m + k, MP) // 2 == g)
+                def _():
+                    copy.start()
+
     grads_t = [dqkv[j].reshape(LW, LW) for j in range(3)]
-    project_back(1, grads_t, wt)
-    rs2 = [scatter_mp(p, 1, rows) for p, rows in zip((4, 10), halves)]
     for j in range(2):
         weight_grad(j, nhall, grads_t[j])
     core_t1 = core_send(0)
@@ -500,6 +524,13 @@
     x_k = core_sum_x_send(3, core_k)
     project_back(2, [dqs[j].reshape(LW, LW) for j in range(3)], ws)
     rs3 = scatter_mp(6, 2)
+    stores = []
+
+    def store(source, target):
+        copy = pltpu.make_async_copy(source, target, out_sem.at[len(stores)])
+        copy.start()
+        stores.append(copy)
+
     x_t2 = z_sum_x_send(1, z_t2)
     z_o = x_sum_z_send(5, x_o)
     z_sum(0, z_t1, [gt_ref.at[0], gt_ref.at[1]])
@@ -507,6 +538,8 @@
     z_q = x_sum_z_send(2, x_q)
     x_sum(1, x_t2, [gt_ref.at[2], gto_ref])
     z_k = x_sum_z_send(3, x_k)
+    store(gt_ref, gt_out)
+    store(gto_ref, gto_out)
     x_v = z_sum_x_send(4, z_v)
     wait_all(rs3)
     for k in range(3):
@@ -514,14 +547,21 @@
     x = x_ref[...].astype(F32)
     inv_x = lax.rsqrt(jnp.mean(x * x, -1, keepdims=True) + EPS)
     tok_ref[...] = (dhid[...] + norm_back(x, inv_x, d_nx)).astype(BF16)
+    store(tok_ref, tok_out)
     z_sum(5, z_o, [gso_ref])
+    store(gso_ref, gso_out)
     x_sum(4, x_v, [gs_ref.at[2]])
+    store(gs_ref.at[2], gs_out.at[2])
     z_sum(2, z_q, [gs_ref.at[0]])
+    store(gs_ref.at[0], gs_out.at[0])
     z_sum(3, z_k, [gs_ref.at[1]])
+    store(gs_ref.at[1], gs_out.at[1])
     for copy in pending:
         copy.wait_send()
     for part in range(3):
         hand_wait(part).wait_send()
+    for copy in stores:
+        copy.wait()
 
 
 def deliver(*refs):
@@ -534,6 +574,12 @@
     vmem = pl.BlockSpec(memory_space=pltpu.VMEM)
     dma = pltpu.SemaphoreType.DMA
     scratch = [
+        pltpu.VMEM((ROWS, D), BF16),
+        pltpu.VMEM((3, 16, LW), F32),
+        pltpu.VMEM((16, LW), F32),
+        pltpu.VMEM((3, 16, LW), F32),
+        pltpu.VMEM((16, LW), F32),
+        dma((7,)),
         pltpu.VMEM((ROWS, D), BF16),
         pltpu.VMEM((ROWS, D), BF16),
         pltpu.VMEM((1, clips), jnp.int32),
@@ -595,7 +641,7 @@
             jax.ShapeDtypeStruct((16, LW), F32),
         ),
         in_specs=[pl.BlockSpec(memory_space=pltpu.HBM)] * 7,
-        out_specs=[vmem] * 5,
+        out_specs=[pl.BlockSpec(memory_space=pl.ANY)] * 5,
         scratch_shapes=scratch,
         compiler_params=pltpu.CompilerParams(
             collective_id=0, has_side_effects=True, vmem_limit_bytes=60 * 1024 * 1024

time: 93.8 us -> 93.9 us (level)
  Pallas kernels: 92.2 us -> 93.2 us
    pallas_call x1, Pallas kernels: 90.5 us -> 91.5 us  [shards(): pl.pallas_call(kernel, out_shape=(jax.ShapeDtypeStruct((ROWS, D), BF16),...]
where the time goes in v8:
time: 93.9 us; the launch traced here: 93.8 us
  Pallas kernels  93.2 us (99%)
    pallas_call x1, Pallas kernels, shards(): pl.pallas_call(kernel, out_shape=(jax.ShapeDtypeStruct((ROWS, D), BF16),...  91.5 us

profile of v8, /device:TPU:8, one launch (start us, length us, event | category | flops | bytes accessed | tf_op | source)
XLA Modules:
  0.0 93.8 jit_solution(15929281029476409474)
XLA Ops:
  0.6 91.5 %shard_map.110 = (bf16[64,1024]{1,0:T(8,128)(2,1)}, f32[3,16,256]{2,1,0:T(8,128)}, f32[16,256]{1,0:T(8,128)}, f32[3,16,256]{2,1,0:T(8,128)}, f32[16,256]{1,0:T(8,128)}) custom-call(bf16[64,1024]{1,0:T(8,128)(2,1)} %bitcast.6, bf16[64,1024]{1,0:T(8,128)(2,1)} %bitcast.7, s32[1,32]{1,0:T(1,128)} %bitcast.11, bf16[3,1024,256]{2,1,0:T(8,128)(2,1)} %ws_hbm.1, ...), custom_call_target="tpu_custom_call" | custom-call | flops 3500000000 | bytes 6000000 | tf_op jit(solution)/shard_map/pallas_call | solution.py:634
  92.2 1.7 %shard_map.111 = (bf16[64,1024]{1,0:T(8,128)(2,1)}, f32[3,16,256]{2,1,0:T(8,128)}, f32[16,256]{1,0:T(8,128)}, f32[3,16,256]{2,1,0:T(8,128)}, f32[16,256]{1,0:T(8,128)}) custom-call(bf16[64,1024]{1,0:T(8,128)(2,1)} %get-tuple-element.15.refs_0_, f32[3,16,256]{2,1,0:T(8,128)} %get-tuple-element.16.refs_1_, f32[16,256]{1,0:T(8,128)} %get-tuple-element.17.refs_2_, ...), custom_call_target="tpu_custom_call" | custom-call | tf_op jit(solution)/shard_map/pallas_call | solution.py:656

commit v9 on v8

--- a/solution.py
+++ b/solution.py
@@ -171,6 +171,7 @@
             tbuf[t, g, used:] = jnp.zeros((16 - used, 16, LW), BF16)
 
     halves = [slice(0, ROWS // 2), slice(ROWS // 2, ROWS)]
+    quarters = [slice(16 * at, 16 * at + 16) for at in range(4)]
     masks = [head_mask(h) for h in range(HEADS_LOC)]
 
     loads[3].wait()
@@ -199,7 +200,7 @@
     for c in range(4):
         cols = pl.ds(c * 256, 256)
         rsend[0, :, :, cols] = dot(attn, wos[:, cols]).astype(BF16).reshape(MP, ROWS, 256)
-    rs1 = [scatter_mp(p, 0, rows) for p, rows in zip((2, 8), halves)]
+    rs1 = [scatter_mp(p, 0, rows) for p, rows in zip((2, 8, 16, 17), quarters)]
     own = dot(attns[m], wos[...])
     for c in range(4):
         x_turned[c] = xall[:, :, c * 256 : (c + 1) * 256].reshape(LW, 256).T
@@ -217,7 +218,7 @@
     pending.extend(far_g)
 
     ag_h = []
-    for at, rows in enumerate(halves):
+    for at, rows in enumerate(quarters):
         for copy in rs1[at]:
             copy.wait_recv()
         hidden = x_ref[rows].astype(F32) + own[rows]
@@ -226,7 +227,7 @@
         inv_h = lax.rsqrt(jnp.mean(hidden * hidden, -1, keepdims=True) + EPS)
         hid[rows] = hidden
         nhall[m, rows] = (hidden * inv_h).astype(BF16)
-        ag_h += gather_mp((3, 9)[at], nhall.at[m], nhall, rows)
+        ag_h += gather_mp((3, 9, 18, 19)[at], nhall.at[m], nhall, rows)
 
     def plane_send(part, source, target, ssems, rsems):
         copies = []
@@ -445,7 +446,7 @@
             out[...] = summed
 
     rs2 = []
-    for phase, rows in zip((4, 10), halves):
+    for phase, rows in zip((4, 10, 12, 13), quarters):
         copies = []
         for k in (1, 3, 2):
             to = lax.rem(m + k, MP)
@@ -484,7 +485,7 @@
     x_t1 = core_sum_x_send(0, core_t1)
     z_t2 = core_sum_z_send(1, core_t2)
     ag_d = []
-    for at, rows in enumerate(halves):
+    for at, rows in enumerate(quarters):
         wait_all(rs2[at])
         d_nh = own[rows]
         for k in range(3):
@@ -494,7 +495,7 @@
         d_hidden = g_ref[rows].astype(F32) + norm_back(hidden, inv_h, d_nh)
         dhid[rows] = d_hidden
         dhall[m, rows] = d_hidden.astype(BF16)
-        ag_d += gather_mp((5, 11)[at], dhall.at[m], dhall, rows)
+        ag_d += gather_mp((5, 11, 14, 15)[at], dhall.at[m], dhall, rows)
     z_t1 = x_sum_z_send(0, x_t1)
     wait_all(ag_d)
 
@@ -616,8 +617,8 @@
         pltpu.VMEM((8, XS, 16, LW), BF16),
         pltpu.VMEM((XS - 1, 8, 16, LW), BF16),
         dma((7,)),
-        dma((12, 3)),
-        dma((12, 3)),
+        dma((20, 3)),
+        dma((20, 3)),
         dma((3, PL - 1)),
         dma((3, PL - 1)),
         dma((3,)),

time: 93.9 us -> 93.5 us (level)
  no operation moved by 1% of the time
where the time goes in v9:
time: 93.5 us; the launch traced here: 93.4 us
  Pallas kernels  92.7 us (99%)
    pallas_call x1, Pallas kernels, shards(): pl.pallas_call(kernel, out_shape=(jax.ShapeDtypeStruct((ROWS, D), BF16),...  91 us

profile of v9, /device:TPU:8, one launch (start us, length us, event | category | flops | bytes accessed | tf_op | source)
XLA Modules:
  0.0 93.4 jit_solution(3305254517279814468)
XLA Ops:
  0.6 91.0 %shard_map.110 = (bf16[64,1024]{1,0:T(8,128)(2,1)}, f32[3,16,256]{2,1,0:T(8,128)}, f32[16,256]{1,0:T(8,128)}, f32[3,16,256]{2,1,0:T(8,128)}, f32[16,256]{1,0:T(8,128)}) custom-call(bf16[64,1024]{1,0:T(8,128)(2,1)} %bitcast.6, bf16[64,1024]{1,0:T(8,128)(2,1)} %bitcast.7, s32[1,32]{1,0:T(1,128)} %bitcast.11, bf16[3,1024,256]{2,1,0:T(8,128)(2,1)} %ws_hbm.1, ...), custom_call_target="tpu_custom_call" | custom-call | flops 3500000000 | bytes 6000000 | tf_op jit(solution)/shard_map/pallas_call | solution.py:635
  91.7 1.7 %shard_map.111 = (bf16[64,1024]{1,0:T(8,128)(2,1)}, f32[3,16,256]{2,1,0:T(8,128)}, f32[16,256]{1,0:T(8,128)}, f32[3,16,256]{2,1,0:T(8,128)}, f32[16,256]{1,0:T(8,128)}) custom-call(bf16[64,1024]{1,0:T(8,128)(2,1)} %get-tuple-element.15.refs_0_, f32[3,16,256]{2,1,0:T(8,128)} %get-tuple-element.16.refs_1_, f32[16,256]{1,0:T(8,128)} %get-tuple-element.17.refs_2_, ...), custom_call_target="tpu_custom_call" | custom-call | tf_op jit(solution)/shard_map/pallas_call | solution.py:657
